TPU v7x, 256 devices: a whole 4x4x8 slice. The times are simulated.
256 devices in a mesh: group: 4 (over x), session: 64 (over z, y, core).
Axes of the slice: x: 4, y: 4, z: 8, core: 2. Of those that a mesh axis runs over, the one named last changes fastest.
Arguments:
- spikes: bfloat16 [98304, 128], P(('group', 'session')), may hold values from -6 to 6
- row_owner: int32 [98304, 1], P(('group', 'session')), may hold values from 0 to 63; in each aligned block of 384 rows (0 to 383, 384 to 767, ...) at most 12 rows name the same one
- row_block: int32 [98304], P(('group', 'session')), may hold values from 0 to 1
- chan_count: int32 [128], P('session'), may hold values from 96 to 128
- readin: bfloat16 [16384, 1024], P('session'), may hold values from -0.5 to 0.5
- readout: bfloat16 [1024, 16384], P(None, 'session'), may hold values from -0.1875 to 0.1875
- first_layer: bfloat16 [1024, 1024], replicated, may hold values from -0.1875 to 0.1875
- second_layer: bfloat16 [1024, 1024], replicated, may hold values from -0.1875 to 0.1875
Outputs:
- rebuilt: bfloat16 [98304, 128], P(('group', 'session'))
- readin_grad: float32 [16384, 1024], P('session')
- readout_grad: float32 [1024, 16384], P(None, 'session')
- first_grad: float32 [1024, 1024], P('session')
- second_grad: float32 [1024, 1024], P('session')
Inputs may be any that keep to these rules, and one draw needn't show every extreme that they name: `row_owner`: among the 384 rows of one device, no owner is named by more than 12 rows, a bound that some block reaches.
All inputs are finite; a program needn't handle non-finite values.
Results may differ from a plain program's by a relative error of at most 0.012.
Values may be sent and summed in bfloat16 or wider, within the bound.
No kernel may reach another device: no remote copies, remote signals or barrier semaphores. Data moves between devices by JAX's collectives and lax.ppermute only.
A program may use at most 64 MiB of HBM per device.

v0:
```python
import jax
import jax.numpy as jnp
from jax import lax
from jax.sharding import PartitionSpec as P


def on_device(spikes, row_owner, row_block, chan_count, readin, readout, first_layer, second_layer):
    row_total, channels = spikes.shape
    owners = lax.axis_size("session")
    capacity = 2 * row_total // owners
    slot_count = owners * capacity
    block_count = chan_count.shape[0]
    owner_ids = row_owner[:, 0]
    matches = (owner_ids[:, None] == jnp.arange(owners, dtype=jnp.int32)[None, :]).astype(jnp.int32)
    before = jnp.cumsum(matches, axis=0) - matches
    target = owner_ids * capacity + jnp.sum(before * matches, axis=1)
    packed = jnp.zeros((slot_count, channels), jnp.bfloat16).at[target].set(spikes)
    labels = jnp.zeros((slot_count,), jnp.int32).at[target].set(row_block + 1)
    got_rows, got_labels = (
        lax.all_to_all(
            packed.reshape(owners, capacity, channels),
            "session",
            split_axis=0,
            concat_axis=0,
            tiled=True,
        ),
        lax.all_to_all(
            labels.reshape(owners, capacity), "session", split_axis=0, concat_axis=0, tiled=True
        ),
    )
    got_rows = got_rows.reshape(slot_count, channels)
    got_labels = got_labels.reshape(slot_count)
    chosen = got_labels[:, None] - 1 == jnp.arange(block_count, dtype=jnp.int32)[None, :]
    counts = jnp.sum(jnp.where(chosen, chan_count[None, :], 0), axis=1)
    visible = jnp.arange(channels, dtype=jnp.int32)[None, :] < counts[:, None]
    inputs = jnp.where(visible, got_rows, jnp.zeros_like(got_rows))
    chosen_b = chosen.astype(jnp.bfloat16)
    spread = (chosen_b[:, :, None] * inputs[:, None, :]).reshape(slot_count, block_count * channels)
    factors = jnp.dot(spread, readin, preferred_element_type=jnp.float32).astype(jnp.bfloat16)
    pre_act = jnp.dot(factors, first_layer, preferred_element_type=jnp.float32)
    activity = jax.nn.silu(pre_act).astype(jnp.bfloat16)
    latent = jnp.dot(activity, second_layer, preferred_element_type=jnp.float32).astype(
        jnp.bfloat16
    )
    wide_rates = jnp.dot(latent, readout, preferred_element_type=jnp.float32)
    rates = jnp.sum(
        chosen.astype(jnp.float32)[:, :, None]
        * wide_rates.reshape(slot_count, block_count, channels),
        axis=1,
    )
    rebuilt_slots = jnp.where(visible, rates, 0.0).astype(jnp.bfloat16)
    returned = lax.all_to_all(
        rebuilt_slots.reshape(owners, capacity, channels),
        "session",
        split_axis=0,
        concat_axis=0,
        tiled=True,
    )
    rebuilt = returned.reshape(slot_count, channels)[target]
    weight = (block_count / row_total) ** 0.5
    errors = (jnp.where(visible, rates - inputs.astype(jnp.float32), 0.0) * weight).astype(
        jnp.bfloat16
    )
    err_wide = (chosen_b[:, :, None] * errors[:, None, :]).reshape(
        slot_count, block_count * channels
    )
    dims_rows = (((0,), (0,)), ((), ()))
    dims_cols = (((1,), (1,)), ((), ()))
    grad_out = lax.dot_general(latent, err_wide, dims_rows, preferred_element_type=jnp.float32)
    d_latent = lax.dot_general(
        err_wide, readout, dims_cols, preferred_element_type=jnp.float32
    ).astype(jnp.bfloat16)
    grad_two = lax.dot_general(activity, d_latent, dims_rows, preferred_element_type=jnp.float32)
    share_two = lax.psum_scatter(grad_two, "session", scatter_dimension=0, tiled=True)
    d_act = lax.dot_general(d_latent, second_layer, dims_cols, preferred_element_type=jnp.float32)
    sigmoid_pre = jax.nn.sigmoid(pre_act)
    d_pre = (d_act * sigmoid_pre * (1.0 + pre_act * (1.0 - sigmoid_pre))).astype(jnp.bfloat16)
    grad_one = lax.dot_general(factors, d_pre, dims_rows, preferred_element_type=jnp.float32)
    share_one = lax.psum_scatter(grad_one, "session", scatter_dimension=0, tiled=True)
    d_factors = lax.dot_general(
        d_pre, first_layer, dims_cols, preferred_element_type=jnp.float32
    ).astype(jnp.bfloat16)
    grad_in = lax.dot_general(spread, d_factors, dims_rows, preferred_element_type=jnp.float32)
    summed_in, summed_out, summed_one, summed_two = (
        lax.psum(grad_in.astype(jnp.bfloat16), "group").astype(jnp.float32),
        lax.psum(grad_out.astype(jnp.bfloat16), "group").astype(jnp.float32),
        lax.psum(share_one.astype(jnp.bfloat16), "group").astype(jnp.float32),
        lax.psum(share_two.astype(jnp.bfloat16), "group").astype(jnp.float32),
    )
    grad_scale = 1.0 / (block_count * owners) ** 0.5
    return (rebuilt, summed_in, summed_out, summed_one * grad_scale, summed_two * grad_scale)


def solution(mesh):
    placed = (
        P(("group", "session"), None),
        P(("group", "session"), None),
        P(("group", "session")),
        P("session"),
        P("session", None),
        P(None, "session"),
        P(),
        P(),
    )
    return jax.shard_map(
        on_device,
        mesh=mesh,
        in_specs=placed,
        out_specs=(
            P(("group", "session"), None),
            P("session", None),
            P(None, "session"),
            P("session", None),
            P("session", None),
        ),
        check_vma=False,
    )
```

profile of v0, /device:TPU:6, one launch (start us, length us, event | category | flops | bytes accessed | tf_op | source)
XLA Modules:
  0.0 412.0 jit_solution(13084813504341246636)
XLA Ops:
  11.6 2.9 scatter_custom_fusion
  15.2 12.1 %all-to-all-start = ((s32[64,1,12]{2,1,0:T(1,128)}), s32[64,1,12]{2,1,0:T(1,128)S(1)}, u32[]{:S(2)}, u32[]{:S(2)}) async-start(s32[64,1,12]{2,1,0:T(1,128)} %bitcast.1), calls=%async_computation | async-start | bytes 65536 | tf_op jit(solution)/shard_map/all_to_all | solution.py:27
  27.3 1.9 scatter_custom_fusion.1
  30.0 6.9 %all-to-all-done = s32[64,1,12]{2,1,0:T(1,128)S(1)} async-done(((s32[64,1,12]{2,1,0:T(1,128)}), s32[64,1,12]{2,1,0:T(1,128)S(1)}, u32[]{:S(2)}, u32[]{:S(2)}) %all-to-all-start) | async-done | bytes 3104 | tf_op jit(solution)/shard_map/all_to_all | solution.py:27
  36.9 4.6 %all-to-all-start.1 = ((bf16[64,12,128]{2,1,0:T(8,128)(2,1)}), bf16[64,12,128]{2,1,0:T(8,128)(2,1)S(1)}, u32[]{:S(2)}, u32[]{:S(2)}) async-start(bf16[64,12,128]{2,1,0:T(8,128)(2,1)} %reshape.157), calls=%async_computation.1 | async-start | bytes 524288 | tf_op jit(solution)/shard_map/all_to_all | solution.py:20
  42.2 12.2 %all-to-all-done.1 = bf16[64,12,128]{2,1,0:T(8,128)(2,1)S(1)} async-done(((bf16[64,12,128]{2,1,0:T(8,128)(2,1)}), bf16[64,12,128]{2,1,0:T(8,128)(2,1)S(1)}, u32[]{:S(2)}, u32[]{:S(2)}) %all-to-all-start.1) | async-done | bytes 196640 | tf_op jit(solution)/shard_map/all_to_all | solution.py:20
  58.2 1.8 fusion.21
  60.1 1.8 convolution_convert_fusion.2
  68.9 3.8 fusion.20
  72.8 4.9 %multiply_convert_fusion = bf16[768,1024]{1,0:T(8,128)(2,1)S(1)} fusion(f32[768,1024]{1,0:T(8,128)} %copy-done.13, bf16[768,1024]{1,0:T(8,128)(2,1)} %copy-done.4, bf16[1024,1024]{1,0:T(8,128)(2,1)S(1)} %copy-done), kind=kOutput, calls=%fused_computation.3 | convolution fusion | flops 1617690624 | bytes 8388608 | tf_op jit(solution)/shard_map/dot_general | solution.py:75
  77.7 1.2 copy-done.15
  78.9 3.8 fusion.23
  83.7 2.9 convolution_convert_fusion.4
  86.5 5.2 %convolution_convert_fusion.5 = bf16[256,1024]{1,0:T(8,128)(2,1)} fusion(bf16[768,1024]{1,0:T(8,128)(2,1)} %copy-done.15, bf16[1024,1024]{1,0:T(8,128)(2,1)} %param.14, bf16[96,8,2,128]{3,2,1,0:T(2,128)(2,1)S(1)} %bitcast.54), kind=kOutput, calls=%fused_computation.11 | convolution fusion | flops 2014314496 | bytes 4587520 | tf_op jit(solution)/shard_map/dot_general | solution.py:83
  92.8 4.9 %all-to-all-start.2 = ((bf16[64,12,128]{2,1,0:T(8,128)(2,1)}), bf16[64,12,128]{2,1,0:T(8,128)(2,1)S(1)}, u32[]{:S(2)}, u32[]{:S(2)}) async-start(bf16[64,12,128]{2,1,0:T(8,128)(2,1)} %select_convert_fusion), calls=%async_computation.2 | async-start | bytes 524288 | tf_op jit(solution)/shard_map/all_to_all | solution.py:52
  97.8 114.7 %reduce-scatter.5.cloned.1.call-done = f32[16,1024]{1,0:T(8,128)} async-done(((f32[1024,1024]{1,0:T(8,128)}), f32[16,1024]{1,0:T(8,128)}) %reduce-scatter.5.cloned.1.call-update) | async-done | bytes 65552 | tf_op jit(solution)/shard_map/reduce_scatter | solution.py:74
  212.5 1.5 convert_element_type.100
  213.9 144.8 %reduce-scatter.3.cloned.1.call-done = f32[16,1024]{1,0:T(8,128)} async-done(((f32[1024,1024]{1,0:T(8,128)}), f32[16,1024]{1,0:T(8,128)}) %reduce-scatter.3.cloned.1.call-update) | async-done | bytes 65552 | tf_op jit(solution)/shard_map/reduce_scatter | solution.py:79
  358.8 1.5 convert_element_type.98
  360.3 1.9 gather_fusion
  362.3 2.1 convert_element_type.95
  364.4 2.1 convert_element_type.97
  366.5 36.7 %all-reduce.5.cloned.1.call-done = (bf16[16,1024]{1,0:T(8,128)(2,1)}, bf16[16,1024]{1,0:T(8,128)(2,1)}) async-done(((bf16[16,1024]{1,0:T(8,128)(2,1)}, bf16[16,1024]{1,0:T(8,128)(2,1)}), (bf16[16,1024]{1,0:T(8,128)(2,1)}, bf16[16,1024]{1,0:T(8,128)(2,1)})) %all-reduce.5.cloned.1.call-update) | async-done | bytes 65552 | tf_op jit(solution)/shard_map/psum | solution.py:87
  403.2 1.4 convert_multiply_fusion
  (71 shorter events, 18.5 us)
Async XLA Ops:
  8.0 52.0 %copy-start = (bf16[1024,1024]{1,0:T(8,128)(2,1)S(1)}, bf16[1024,1024]{1,0:T(8,128)(2,1)}, u32[]{:S(2)}) copy-start(bf16[1024,1024]{1,0:T(8,128)(2,1)} %param.15) | copy-start | bytes 6291460
  8.0 34.1 %copy-start.11 = (s32[2]{0:T(128)S(1)}, s32[2]{0:T(128)}, u32[]{:S(2)}) copy-start(s32[2]{0:T(128)} %param.11) | copy-start | bytes 28
  8.0 48.5 %copy-start.10 = (bf16[256,1024]{1,0:T(8,128)(2,1)S(1)}, bf16[256,1024]{1,0:T(8,128)(2,1)}, u32[]{:S(2)}) copy-start(bf16[256,1024]{1,0:T(8,128)(2,1)} %param.12) | copy-start | bytes 1572868
  15.2 21.6 %all-to-all-start = ((s32[64,1,12]{2,1,0:T(1,128)}), s32[64,1,12]{2,1,0:T(1,128)S(1)}, u32[]{:S(2)}, u32[]{:S(2)}) async-start(s32[64,1,12]{2,1,0:T(1,128)} %bitcast.1), calls=%async_computation | async-start | bytes 65536 | tf_op jit(solution)/shard_map/all_to_all | solution.py:27
  36.9 17.6 %all-to-all-start.1 = ((bf16[64,12,128]{2,1,0:T(8,128)(2,1)}), bf16[64,12,128]{2,1,0:T(8,128)(2,1)S(1)}, u32[]{:S(2)}, u32[]{:S(2)}) async-start(bf16[64,12,128]{2,1,0:T(8,128)(2,1)} %reshape.157), calls=%async_computation.1 | async-start | bytes 524288 | tf_op jit(solution)/shard_map/all_to_all | solution.py:20
  41.5 171.0 %reduce-scatter.5.cloned.1.call-start = ((), (), s32[]{:S(2)}) async-start(), calls=%async_computation.6 | async-start | bytes 4259840 | tf_op jit(solution)/shard_map/reduce_scatter | solution.py:74
  54.5 3.7 copy-start.12
  55.7 0.8 copy-start.5
  57.1 1.1 copy-start.2
  60.0 1.9 copy-start.13
  60.1 1.9 copy-start.1
  61.9 1.2 copy-start.9
  65.1 3.7 copy-start.14
  66.3 0.7 copy-start.7
  67.7 1.2 copy-start.4
  72.7 286.1 %reduce-scatter.3.cloned.1.call-start = ((), (), s32[]{:S(2)}) async-start(), calls=%async_computation.5 | async-start | bytes 4259840 | tf_op jit(solution)/shard_map/reduce_scatter | solution.py:79
  72.8 6.1 %copy-start.3 = (bf16[768,1024]{1,0:T(8,128)(2,1)S(1)}, bf16[768,1024]{1,0:T(8,128)(2,1)}, u32[]{:S(2)}) copy-start(bf16[768,1024]{1,0:T(8,128)(2,1)} %copy-done.2) | copy-start | bytes 4718596
  77.7 1.2 copy-start.15
  82.7 1.0 copy-start.8
  82.7 3.9 copy-start.6
  82.7 279.6 %all-reduce.7.cloned.1.call-start = ((), (), s32[]{:S(2)}) async-start(), calls=%async_computation.8 | async-start | bytes 2097152 | tf_op jit(solution)/shard_map/psum | solution.py:85
  92.8 267.5 %all-to-all-start.2 = ((bf16[64,12,128]{2,1,0:T(8,128)(2,1)}), bf16[64,12,128]{2,1,0:T(8,128)(2,1)S(1)}, u32[]{:S(2)}, u32[]{:S(2)}) async-start(bf16[64,12,128]{2,1,0:T(8,128)(2,1)} %select_convert_fusion), calls=%async_computation.2 | async-start | bytes 524288 | tf_op jit(solution)/shard_map/all_to_all | solution.py:52
  97.7 305.5 %all-reduce.5.cloned.1.call-start = ((), (), s32[]{:S(2)}) async-start(), calls=%async_computation.7 | async-start | bytes 131072 | tf_op jit(solution)/shard_map/psum | solution.py:87
Sparse Core Ops, SparseCore 0:
  72.8 139.6 reduce-scatter.4
  216.6 142.1 reduce-scatter.2
Sparse Core Ops, SparseCore 1:
  91.8 45.8 all-reduce.6
  360.3 42.8 all-reduce.4
where the time goes:
time: 414 us; the launch traced here: 412 us
  waiting for transfers between devices  315 us (76%)
  matrix products  26 us (6%)
  starting transfers between devices  22.2 us (5%)
  local copies, waits for them, and re-layouts  16.4 us (4%)
  other arithmetic  16.1 us (4%)
  between operations  15.9 us (4%)
    reduce_scatter x1, waiting for transfers between devices, on_device(): lax.psum_scatter(grad_one, 'session', scatter_dimension=0, tiled=True)  145 us
    reduce_scatter x1, waiting for transfers between devices, on_device(): lax.psum_scatter(grad_two, 'session', scatter_dimension=0, tiled=True)  115 us
    psum x1, waiting for transfers between devices, on_device(): lax.psum(share_one.astype(jnp.bfloat16), 'group').astype(jnp.float32)  36.7 us
    all_to_all x1, waiting for transfers between devices, on_device(): lax.all_to_all(packed.reshape(owners, capacity, channels), 'session', spl...  12.2 us
    all_to_all x1, starting transfers between devices, on_device(): lax.all_to_all(labels.reshape(owners, capacity), 'session', split_axis=0,...  12.1 us
  transfers between devices with their start and end apart: 7, of which 5 were waited for; matrix products, arithmetic and copies ran while one was open for 7% of the time, Pallas kernels for 0%

commit v1 on v0

v1 whole, which is shorter than its diff:
```python
import functools

import jax
import jax.numpy as jnp
from jax import lax
from jax.experimental import pallas as pl
from jax.experimental.pallas import tpu as pltpu
from jax.sharding import Mesh, PartitionSpec as P

ZS, YS, CS = 8, 4, 2
CH = 128
STRIDE = 16
CAP = 12
TILE = 256
BF = jnp.bfloat16
F32 = jnp.float32
ROWS_DIMS = (((0,), (0,)), ((), ()))
COLS_DIMS = (((1,), (1,)), ((), ()))


def dot(a, b):
    return jnp.dot(a, b, preferred_element_type=F32)


def dot_rows(a, b):
    return lax.dot_general(a, b, ROWS_DIMS, preferred_element_type=F32)


def dot_cols(a, b):
    return lax.dot_general(a, b, COLS_DIMS, preferred_element_type=F32)


def iota(shape, dim):
    return lax.broadcasted_iota(jnp.int32, shape, dim)


def pack_kernel(owner_ref, block_ref, spikes_ref, packed_ref, target_ref):
    rows = spikes_ref.shape[0]
    slots = packed_ref.shape[0]
    owner = owner_ref[...]
    match = owner == iota((rows, CH), 1)
    earlier = (iota((rows, rows), 1) < iota((rows, rows), 0)).astype(BF)
    before = dot(earlier, match.astype(F32).astype(BF))
    rank = jnp.sum(jnp.where(match, before, 0.0), axis=1, keepdims=True).astype(jnp.int32)
    target = owner * STRIDE + rank
    target_ref[...] = target
    label = (block_ref[...] + 1).astype(F32)
    label_rows = jnp.where(iota((rows, CH), 1) == rank, label, 0.0).astype(BF)
    slot_ids = iota((rows, slots), 1)
    place = (slot_ids == target).astype(F32).astype(BF)
    label_place = (slot_ids == owner * STRIDE + CAP).astype(F32).astype(BF)
    packed_ref[...] = (dot_rows(place, spikes_ref[...]) + dot_rows(label_place, label_rows)).astype(BF)


def unpack_kernel(target_ref, back_ref, rebuilt_ref):
    rows = rebuilt_ref.shape[0]
    slots = back_ref.shape[0]
    place = (iota((rows, slots), 1) == target_ref[...]).astype(F32).astype(BF)
    rebuilt_ref[...] = dot(place, back_ref[...]).astype(BF)


def split_pair(core, tile, send_ref, own_ref, at):
    cols = tile.shape[1]
    first = core == 0
    for j in range(8):
        low, high = tile[32 * j : 32 * j + 16], tile[32 * j + 16 : 32 * j + 32]
        z, y = at * 2 + j // 4, j % 4
        send_ref[y, z] = jnp.where(first, high, low).astype(BF)
        own_ref[y, z] = jnp.where(first, low, high).astype(BF)


def forward_kernel(weight, core_ref, count_ref, got_ref, win_ref, wout_ref, one_ref, two_ref,
                   slots_ref, gout_ref, spread_ref, factors_ref, pre_ref, dlat_ref, send_ref, own_ref,
                   act_ref, lat_ref, err_ref, lab_ref, reb_ref):
    rows = spread_ref.shape[0]
    per, wide = 16 * CAP, 16 * STRIDE
    row, col = iota((per, wide), 0), iota((per, wide), 1)
    source = (row * 5462) >> 16
    pick = (col == source * STRIDE + row - source * CAP).astype(F32).astype(BF)
    pick_label = (col == source * STRIDE + CAP).astype(F32).astype(BF)
    row1, lane = iota((per, CH), 0), iota((per, CH), 1)
    rank1 = row1 - ((row1 * 5462) >> 16) * CAP
    for b in range(rows // per):
        block = got_ref[b * wide : (b + 1) * wide]
        taken = dot(pick, block)
        label = jnp.sum(jnp.where(lane == rank1, dot(pick_label, block), 0.0), axis=1, keepdims=True)
        counts = jnp.where(label == 1.0, count_ref[0], jnp.where(label == 2.0, count_ref[1], 0))
        inputs = jnp.where(lane < counts, taken, 0.0)
        here = pl.ds(b * per, per)
        lab_ref[here] = label
        spread_ref[here, :CH] = jnp.where(label == 1.0, inputs, 0.0).astype(BF)
        spread_ref[here, CH:] = jnp.where(label == 2.0, inputs, 0.0).astype(BF)

    def step(t, carry):
        here = pl.ds(pl.multiple_of(t * TILE, TILE), TILE)
        spread = spread_ref[here]
        factors = dot(spread, win_ref[...]).astype(BF)
        factors_ref[here] = factors
        pre = dot(factors, one_ref[...])
        pre_ref[here] = pre
        act = (pre / (1.0 + jnp.exp(-pre))).astype(BF)
        act_ref[here] = act
        lat = dot(act, two_ref[...]).astype(BF)
        lat_ref[here] = lat
        both = dot(lat, wout_ref[...])
        label = lab_ref[here]
        is0, is1 = label == 1.0, label == 2.0
        counts = jnp.where(is0, count_ref[0], jnp.where(is1, count_ref[1], 0))
        visible = iota((TILE, CH), 1) < counts
        rates = jnp.where(is0, both[:, :CH], both[:, CH:])
        rates = jnp.where(visible, rates, 0.0)
        reb_ref[here] = rates.astype(BF)
        inputs = spread[:, :CH].astype(F32) + spread[:, CH:].astype(F32)
        errors = ((rates - inputs) * weight)
        err = jnp.concatenate([jnp.where(is0, errors, 0.0), jnp.where(is1, errors, 0.0)], axis=1).astype(BF)
        err_ref[here] = err
        dlat_ref[here] = dot_cols(err, wout_ref[...]).astype(BF)
        return carry

    lax.fori_loop(0, rows // TILE, step, 0)
    core = core_ref[0]

    def grads(m, carry):
        cols = pl.ds(pl.multiple_of(m * TILE, TILE), TILE)
        gout_ref[m] = dot_rows(lat_ref[:, cols], err_ref[...]).astype(BF)
        split_pair(core, dot_rows(act_ref[:, cols], dlat_ref[...]), send_ref, own_ref, m)
        return carry

    lax.fori_loop(0, 4, grads, 0)
    for b in range(rows // per):
        slots_ref[b * wide : (b + 1) * wide] = dot_rows(pick, reb_ref[b * per : (b + 1) * per]).astype(BF)


def inner_kernel(core_ref, dlat_ref, two_ref, pre_ref, factors_ref, dpre_ref, send_ref, own_ref):
    rows = dpre_ref.shape[0]

    def step(t, carry):
        here = pl.ds(pl.multiple_of(t * TILE, TILE), TILE)
        dact = dot_cols(dlat_ref[here], two_ref[...])
        pre = pre_ref[here]
        s = 1.0 / (1.0 + jnp.exp(-pre))
        dpre_ref[here] = (dact * s * (1.0 + pre * (1.0 - s))).astype(BF)
        return carry

    lax.fori_loop(0, rows // TILE, step, 0)
    core = core_ref[0]

    def grads(m, carry):
        cols = pl.ds(pl.multiple_of(m * TILE, TILE), TILE)
        split_pair(core, dot_rows(factors_ref[:, cols], dpre_ref[...]), send_ref, own_ref, m)
        return carry

    lax.fori_loop(0, 4, grads, 0)


def readin_kernel(dpre_ref, one_ref, spread_ref, gin_ref, dfac_ref):
    rows = dpre_ref.shape[0]

    def step(t, carry):
        here = pl.ds(pl.multiple_of(t * TILE, TILE), TILE)
        dfac_ref[here] = dot_cols(dpre_ref[here], one_ref[...]).astype(BF)
        return carry

    lax.fori_loop(0, rows // TILE, step, 0)
    grad = dot_rows(spread_ref[...], dfac_ref[...]).astype(BF)
    for j in range(4):
        gin_ref[j] = grad[64 * j : 64 * j + 64]


VM = pl.BlockSpec(memory_space=pltpu.VMEM)
SM = pl.BlockSpec(memory_space=pltpu.SMEM)


def call(kernel, outs, *args, smem=0, scratch=(), flops=0, moved=0):
    return pl.pallas_call(
        kernel,
        out_shape=[jax.ShapeDtypeStruct(s, d) for s, d in outs],
        in_specs=[SM] * smem + [VM] * (len(args) - smem),
        out_specs=[VM] * len(outs),
        scratch_shapes=[pltpu.VMEM(s, d) for s, d in scratch],
        compiler_params=pltpu.CompilerParams(vmem_limit_bytes=56 * 1024 * 1024),
        cost_estimate=pl.CostEstimate(flops=flops, bytes_accessed=moved, transcendentals=0),
    )(*args)


def ring(n, k):
    return [(i, (i + k) % n) for i in range(n)]


def pick_at(x, i, axis=0):
    return lax.dynamic_index_in_dim(x, i, axis, keepdims=False)


def scatter_sum(x, axis, n):
    me = lax.axis_index(axis)
    got = [
        lax.ppermute(pick_at(x, (me + k) % n).astype(BF), axis, ring(n, k)) for k in range(1, n)
    ]
    total = pick_at(x, me).astype(F32)
    for g in got:
        total = total + g.astype(F32)
    return total


def gather(x, axis, n):
    me = lax.axis_index(axis)
    got = [x] + [lax.ppermute(x, axis, ring(n, k)) for k in range(1, n)]
    parts = []
    for j in range(n):
        part = got[0]
        for k in range(1, n):
            part = jnp.where((me - k) % n == j, got[k], part)
        parts.append(part)
    return jnp.stack(parts)


def all_sum(x, axis):
    x = x.astype(BF)
    a, b, c = [lax.ppermute(x, axis, ring(4, k)).astype(F32) for k in (1, 2, 3)]
    return (x.astype(F32) + b) + (a + c)


def layer_share(send, own):
    got = lax.ppermute(send, "core", ring(CS, 1))
    chip = own.astype(F32) + got.astype(F32)
    mine = scatter_sum(chip, "y", YS)
    parts = lax.all_to_all(mine.astype(BF), "z", split_axis=0, concat_axis=0, tiled=True)
    return jnp.sum(parts.astype(F32), axis=0)


def on_device(spikes, row_owner, row_block, chan_count, readin, readout, first_layer, second_layer):
    session = ("z", "y", "core")
    rows = spikes.shape[0]
    owners = ZS * YS * CS
    slots, count = owners * STRIDE, owners * CAP
    lat = readin.shape[1]
    core = lax.axis_index("core").astype(jnp.int32).reshape(1)
    packed, target = call(
        pack_kernel, [((slots, CH), BF), ((rows, 1), jnp.int32)], row_owner, row_block[:, None], spikes
    )
    got = lax.all_to_all(packed, session, split_axis=0, concat_axis=0, tiled=True)
    weight = (chan_count.shape[0] / rows) ** 0.5
    pair = [((YS, ZS, 16, lat), BF)] * 2
    back, gout, spread, factors, pre, dlat, send2, own2 = call(
        functools.partial(forward_kernel, weight),
        [((slots, CH), BF), ((4, TILE, TILE), BF), ((count, TILE), BF), ((count, lat), BF), ((count, lat), F32),
         ((count, lat), BF)] + pair,
        core, chan_count, got, readin, readout, first_layer, second_layer,
        smem=2,
        scratch=[((count, lat), BF), ((count, lat), BF), ((count, TILE), BF), ((count, 1), F32), ((count, CH), BF)],
        flops=7_000_000_000, moved=16_000_000,
    )
    dpre, send1, own1 = call(
        inner_kernel, [((count, lat), BF)] + pair, core, dlat, second_layer, pre, factors,
        smem=1, flops=3_200_000_000, moved=12_000_000,
    )
    (gin,) = call(
        readin_kernel, [((4, 64, lat), BF)], dpre, first_layer, spread,
        scratch=[((count, lat), BF)], flops=2_000_000_000, moved=5_000_000,
    )
    share2 = layer_share(send2, own2)
    share1 = layer_share(send1, own1)
    scale = 1.0 / (chan_count.shape[0] * owners) ** 0.5
    both = all_sum(jnp.stack([share1, share2]), "group") * scale
    out_sum = gather(scatter_sum(gout, "group", 4).astype(BF), "group", 4).astype(F32).reshape(lat, TILE)
    in_sum = gather(scatter_sum(gin, "group", 4).astype(BF), "group", 4).astype(F32).reshape(TILE, lat)
    returned = lax.all_to_all(back, session, split_axis=0, concat_axis=0, tiled=True)
    (rebuilt,) = call(unpack_kernel, [((rows, CH), BF)], target, returned)
    return rebuilt, in_sum, out_sum, both[0], both[1]


def solution(mesh):
    groups = mesh.shape["group"]
    fine = Mesh(mesh.devices.reshape(groups, ZS, YS, CS), ("group", "z", "y", "core"))
    session = ("z", "y", "core")
    rows = ("group",) + session
    return jax.shard_map(
        on_device,
        mesh=fine,
        in_specs=(P(rows, None), P(rows, None), P(rows), P(session), P(session, None), P(None, session), P(), P()),
        out_specs=(P(rows, None), P(session, None), P(None, session), P(session, None), P(session, None)),
        check_vma=False,
    )
```

time: 414 us -> 151 us (0.36)
  the two profiles are of different devices: /device:TPU:6 before, /device:TPU:1 now
where the time goes in v1:
time: 151 us; the launch traced here: 150 us
  starting transfers between devices  61.4 us (41%)
  waiting for transfers between devices  36.1 us (24%)
  Pallas kernels  36 us (24%)
  other arithmetic  8.43 us (6%)
  local copies, waits for them, and re-layouts  7.18 us (5%)
    pallas_call x5, Pallas kernels, call(): pl.pallas_call(kernel, out_shape=[jax.ShapeDtypeStruct(s, d) for s, d in...  36 us
    ppermute x12, starting transfers between devices, scatter_sum(): lax.ppermute(pick_at(x, (me + k) % n).astype(BF), axis, ring(n, k))  15 us
    all_to_all x1, starting transfers between devices, on_device(): lax.all_to_all(back, session, split_axis=0, concat_axis=0, tiled=True)  14.3 us
    all_to_all x1, waiting for transfers between devices, on_device(): lax.all_to_all(packed, session, split_axis=0, concat_axis=0, tiled=True)  13.2 us
    all_to_all x1, starting transfers between devices, on_device(): lax.all_to_all(packed, session, split_axis=0, concat_axis=0, tiled=True)  13.2 us
    all_to_all x2, starting transfers between devices, layer_share(): lax.all_to_all(mine.astype(BF), 'z', split_axis=0, concat_axis=0, tiled=T...  9.91 us
    all_to_all x1, waiting for transfers between devices, on_device(): lax.all_to_all(back, session, split_axis=0, concat_axis=0, tiled=True)  8.98 us
    all_to_all x2, waiting for transfers between devices, layer_share(): lax.all_to_all(mine.astype(BF), 'z', split_axis=0, concat_axis=0, tiled=T...  7.05 us
  transfers between devices with their start and end apart: 27, of which 6 were waited for; matrix products, arithmetic and copies ran while one was open for 7% of the time, Pallas kernels for 12%

profile of v1, /device:TPU:1, one launch (start us, length us, event | category | flops | bytes accessed | tf_op | source)
XLA Modules:
  0.0 149.9 jit_solution(6750139849290367018)
XLA Ops:
  0.6 1.5 %copy.14.owner_ref = s32[384,1]{1,0:T(8,128)} copy(s32[384,1]{0,1:T(1,128)} %param.9) | data formatting | bytes 3072 | tf_op args[1]
  3.6 2.8 %shard_map.119 = (bf16[1024,128]{1,0:T(8,128)(2,1)}, s32[384,1]{1,0:T(8,128)}) custom-call(s32[384,1]{1,0:T(8,128)} %copy.14.owner_ref, s32[384,1]{1,0:T(8,128)} %broadcast_in_dim.4.block_ref, bf16[384,128]{1,0:T(8,128)(2,1)} %spikes_ref.1), custom_call_target="tpu_custom_call" | custom-call | tf_op jit(solution)/shard_map/pallas_call | solution.py:175
  6.4 13.2 %all-to-all-start = ((bf16[64,16,128]{2,1,0:T(8,128)(2,1)}), bf16[64,16,128]{2,1,0:T(8,128)(2,1)S(1)}, u32[]{:S(2)}, u32[]{:S(2)}) async-start(bf16[64,16,128]{2,1,0:T(8,128)(2,1)} %bitcast.85), calls=%async_computation | async-start | bytes 524288 | tf_op jit(solution)/shard_map/all_to_all | solution.py:241
  19.6 13.2 %all-to-all-done = bf16[64,16,128]{2,1,0:T(8,128)(2,1)S(1)} async-done(((bf16[64,16,128]{2,1,0:T(8,128)(2,1)}), bf16[64,16,128]{2,1,0:T(8,128)(2,1)S(1)}, u32[]{:S(2)}, u32[]{:S(2)}) %all-to-all-start) | async-done | bytes 262176 | tf_op jit(solution)/shard_map/all_to_all | solution.py:241
  33.5 15.3 %shard_map.120 = (bf16[1024,128]{1,0:T(8,128)(2,1)}, bf16[4,256,256]{2,1,0:T(8,128)(2,1)}, bf16[768,256]{1,0:T(8,128)(2,1)}, bf16[768,1024]{1,0:T(8,128)(2,1)}, ...) custom-call(s32[1]{0:T(128)} %bitcast.core_ref, ...), custom_call_target="tpu_custom_call" | custom-call | flops 7000000000 | bytes 16000000 | tf_op jit(solution)/shard_map/pallas_call | solution.py:175
  49.1 10.0 %shard_map.122 = (bf16[768,1024]{1,0:T(8,128)(2,1)}, bf16[4,8,16,1024]{3,2,1,0:T(8,128)(2,1)}, bf16[4,8,16,1024]{3,2,1,0:T(8,128)(2,1)}) custom-call(s32[1]{0:T(128)} %bitcast.core_ref, bf16[768,1024]{1,0:T(8,128)(2,1)} %get-tuple-element.21.dlat_ref, bf16[1024,1024]{1,0:T(8,128)(2,1)} %two_ref.3, f32[768,1024]{1,0:T(8,128)} %get-tuple-element.22.pre_ref, ...), custom_call_target="tpu_custom_call" | custom-call | flops 3200000000 | bytes 12000000 | tf_op jit(solution)/shard_map/pallas_call | solution.py:175
  62.1 1.5 %collective-permute-start.7 = (bf16[256,256]{1,0:T(8,128)(2,1)S(1)}, bf16[256,256]{1,0:T(8,128)(2,1)S(1)}, u32[]{:S(2)}, u32[]{:S(2)}) collective-permute-start(bf16[256,256]{1,0:T(8,128)(2,1)S(1)} %get-tuple-element.43), channel_id=1, source_target_pairs={{0,128},{64,192},{128,0},{192,64},{1,129},{65,193},{129,1},{193,65... | collective-permute-start | bytes 393224 | tf_op jit(solution)/shard_map/ppermute | solution.py:197
  63.6 5.7 %shard_map.123 = bf16[4,64,1024]{2,1,0:T(8,128)(2,1)} custom-call(bf16[768,1024]{1,0:T(8,128)(2,1)} %get-tuple-element.24.dpre_ref, bf16[1024,1024]{1,0:T(8,128)(2,1)} %one_ref.3, bf16[768,256]{1,0:T(8,128)(2,1)} %get-tuple-element.25.spread_ref), custom_call_target="tpu_custom_call" | custom-call | flops 2000000000 | bytes 5000000 | tf_op jit(solution)/shard_map/pallas_call | solution.py:175
  69.3 1.9 %dynamic-slice_bitcast_fusion.5 = (bf16[64,1024]{1,0:T(8,128)(2,1)S(1)}, bf16[64,1024]{1,0:T(8,128)(2,1)}, bf16[64,1024]{1,0:T(8,128)(2,1)}) fusion(bf16[4,64,1024]{2,1,0:T(8,128)(2,1)} %shard_map.123, s32[]{:T(128)S(6)} %select_n.280, s32[]{:T(128)S(6)} %select_n.284, s32[]{:T(128)S(6)} %select_n.282), kind=kLoop, calls=%fused_computation.48 | loop fusion | bytes 786444 | tf_op jit(solution)/shard_map/jit(dynamic_index_in_dim)/squeeze | solution.py:191
  71.5 2.4 %collective-permute-start.2 = (bf16[64,1024]{1,0:T(8,128)(2,1)}, bf16[64,1024]{1,0:T(8,128)(2,1)}, u32[]{:S(2)}, u32[]{:S(2)}) collective-permute-start(bf16[64,1024]{1,0:T(8,128)(2,1)} %get-tuple-element.49), channel_id=1, source_target_pairs={{0,192},{64,0},{128,64},{192,128},{1,193},{65,1},{129,65},{193,129... | collective-permute-start | bytes 393224 | tf_op jit(solution)/shard_map/ppermute | solution.py:197
  75.1 2.2 %collective-permute-start.19 = (bf16[8,16,1024]{2,1,0:T(8,128)(2,1)S(1)}, bf16[8,16,1024]{2,1,0:T(8,128)(2,1)S(1)}, u32[]{:S(2)}, u32[]{:S(2)}) collective-permute-start(bf16[8,16,1024]{2,1,0:T(8,128)(2,1)S(1)} %get-tuple-element.35), channel_id=1, source_target_pairs={{0,6},{2,0},{4,2},{6,4},{1,7},{3,1},{5,3},{7,5},{8,14},{10,8},{12,... | collective-permute-start | bytes 786440 | tf_op jit(solution)/shard_map/ppermute | solution.py:197
  78.7 3.4 %collective-permute-done.17 = bf16[8,16,1024]{2,1,0:T(8,128)(2,1)S(1)} collective-permute-done((bf16[8,16,1024]{2,1,0:T(8,128)(2,1)S(1)}, bf16[8,16,1024]{2,1,0:T(8,128)(2,1)S(1)}, u32[]{:S(2)}, u32[]{:S(2)}) %collective-permute-start.17) | collective-permute-done | bytes 262176 | tf_op jit(solution)/shard_map/ppermute | solution.py:197
  82.0 3.7 %collective-permute-start.15 = (bf16[8,16,1024]{2,1,0:T(8,128)(2,1)S(1)}, bf16[8,16,1024]{2,1,0:T(8,128)(2,1)}, u32[]{:S(2)}, u32[]{:S(2)}) collective-permute-start(bf16[8,16,1024]{2,1,0:T(8,128)(2,1)S(1)} %get-tuple-element.32), channel_id=1, source_target_pairs={{0,6},{2,0},{4,2},{6,4},{1,7},{3,1},{5,3},{7,5},{8,14},{10,8},{12,... | collective-permute-start | bytes 786440 | tf_op jit(solution)/shard_map/ppermute | solution.py:197
  85.7 1.8 %collective-permute-done.18 = bf16[8,16,1024]{2,1,0:T(8,128)(2,1)S(1)} collective-permute-done((bf16[8,16,1024]{2,1,0:T(8,128)(2,1)S(1)}, bf16[8,16,1024]{2,1,0:T(8,128)(2,1)S(1)}, u32[]{:S(2)}, u32[]{:S(2)}) %collective-permute-start.18) | collective-permute-done | bytes 262176 | tf_op jit(solution)/shard_map/ppermute | solution.py:197
  89.2 3.4 %all-to-all-start.3 = ((bf16[8,16,1024]{2,1,0:T(8,128)(2,1)}), bf16[8,16,1024]{2,1,0:T(8,128)(2,1)S(1)}, u32[]{:S(2)}, u32[]{:S(2)}) async-start(bf16[8,16,1024]{2,1,0:T(8,128)(2,1)} %fusion.2), calls=%async_computation.3 | async-start | bytes 524288 | tf_op jit(solution)/shard_map/all_to_all | solution.py:227
  97.3 1.6 %collective-permute-done.14 = bf16[8,16,1024]{2,1,0:T(8,128)(2,1)} collective-permute-done((bf16[8,16,1024]{2,1,0:T(8,128)(2,1)S(1)}, bf16[8,16,1024]{2,1,0:T(8,128)(2,1)}, u32[]{:S(2)}, u32[]{:S(2)}) %collective-permute-start.14) | collective-permute-done | bytes 262176 | tf_op jit(solution)/shard_map/ppermute | solution.py:197
  99.1 2.0 %fusion.5 = bf16[8,16,1024]{2,1,0:T(8,128)(2,1)} fusion(bf16[8,16,1024]{2,1,0:T(8,128)(2,1)} %collective-permute-done.15, bf16[8,16,1024]{2,1,0:T(8,128)(2,1)} %collective-permute-done.14, bf16[8,16,1024]{2,1,0:T(8,128)(2,1)} %collective-permute-done.13, f32[4,8,16,1024]{3,2,1,0:T(8,128)S(1)} %convert_add_fusion.1, s32[]{:T(128)S(6)} %select_n.334), kind=kLoop, calls=%fused_computation.13 | loop fusion | flops 917504 | bytes 1572868 | tf_op jit(solution)/shard_map/convert_element_type | solution.py:227
  101.0 2.0 %collective-permute-start.3 = (bf16[64,1024]{1,0:T(8,128)(2,1)S(1)}, bf16[64,1024]{1,0:T(8,128)(2,1)S(1)}, u32[]{:S(2)}, u32[]{:S(2)}) collective-permute-start(bf16[64,1024]{1,0:T(8,128)(2,1)S(1)} %fusion.17), channel_id=1, source_target_pairs={{0,192},{64,0},{128,64},{192,128},{1,193},{65,1},{129,65},{193,129... | collective-permute-start | bytes 393224 | tf_op jit(solution)/shard_map/ppermute | solution.py:207
  103.0 6.5 %all-to-all-start.2 = ((bf16[8,16,1024]{2,1,0:T(8,128)(2,1)}), bf16[8,16,1024]{2,1,0:T(8,128)(2,1)S(1)}, u32[]{:S(2)}, u32[]{:S(2)}) async-start(bf16[8,16,1024]{2,1,0:T(8,128)(2,1)} %fusion.5), calls=%async_computation.2 | async-start | bytes 524288 | tf_op jit(solution)/shard_map/all_to_all | solution.py:227
  111.8 7.1 %all-to-all-done.2 = bf16[8,16,1024]{2,1,0:T(8,128)(2,1)S(1)} async-done(((bf16[8,16,1024]{2,1,0:T(8,128)(2,1)}), bf16[8,16,1024]{2,1,0:T(8,128)(2,1)S(1)}, u32[]{:S(2)}, u32[]{:S(2)}) %all-to-all-start.2) | async-done | bytes 262176 | tf_op jit(solution)/shard_map/all_to_all | solution.py:227
  118.8 14.3 %all-to-all-start.1 = ((bf16[64,16,128]{2,1,0:T(8,128)(2,1)}), bf16[64,16,128]{2,1,0:T(8,128)(2,1)S(1)}, u32[]{:S(2)}, u32[]{:S(2)}) async-start(bf16[64,16,128]{2,1,0:T(8,128)(2,1)} %bitcast.3), calls=%async_computation.1 | async-start | bytes 524288 | tf_op jit(solution)/shard_map/all_to_all | solution.py:267
  134.4 1.8 %collective-permute-start.22 = (bf16[2,16,1024]{2,1,0:T(8,128)(2,1)S(1)}, bf16[2,16,1024]{2,1,0:T(8,128)(2,1)S(1)}, u32[]{:S(2)}, u32[]{:S(2)}) collective-permute-start(bf16[2,16,1024]{2,1,0:T(8,128)(2,1)S(1)} %pad_maximum_fusion.2), channel_id=1, source_target_pairs={{0,192},{64,0},{128,64},{192,128},{1,193},{65,1},{129,65},{193,129... | collective-permute-start | bytes 196616 | tf_op jit(solution)/shard_map/ppermute | solution.py:219
  137.3 9.0 %all-to-all-done.1 = bf16[64,16,128]{2,1,0:T(8,128)(2,1)S(1)} async-done(((bf16[64,16,128]{2,1,0:T(8,128)(2,1)}), bf16[64,16,128]{2,1,0:T(8,128)(2,1)S(1)}, u32[]{:S(2)}, u32[]{:S(2)}) %all-to-all-start.1) | async-done | bytes 262176 | tf_op jit(solution)/shard_map/all_to_all | solution.py:267
  147.0 2.2 %shard_map.121 = bf16[384,128]{1,0:T(8,128)(2,1)} custom-call(s32[384,1]{1,0:T(8,128)} %get-tuple-element.18.target_ref, bf16[1024,128]{1,0:T(8,128)(2,1)} %bitcast.79), custom_call_target="tpu_custom_call" | custom-call | tf_op jit(solution)/shard_map/pallas_call | solution.py:175
  (70 shorter events, 20.9 us)
Async XLA Ops:
  6.4 26.3 %all-to-all-start = ((bf16[64,16,128]{2,1,0:T(8,128)(2,1)}), bf16[64,16,128]{2,1,0:T(8,128)(2,1)S(1)}, u32[]{:S(2)}, u32[]{:S(2)}) async-start(bf16[64,16,128]{2,1,0:T(8,128)(2,1)} %bitcast.85), calls=%async_computation | async-start | bytes 524288 | tf_op jit(solution)/shard_map/all_to_all | solution.py:241
  48.7 25.2 %collective-permute-start.16 = (bf16[4,8,16,1024]{3,2,1,0:T(8,128)(2,1)}, bf16[4,8,16,1024]{3,2,1,0:T(8,128)(2,1)S(1)}, u32[]{:S(2)}, u32[]{:S(2)}) collective-permute-start(bf16[4,8,16,1024]{3,2,1,0:T(8,128)(2,1)} %get-tuple-element.30), channel_id=1, source_target_pairs={{0,1},{1,0},{2,3},{3,2},{4,5},{5,4},{6,7},{7,6},{8,9},{9,8},{10,11... | collective-permute-start | bytes 3145736 | tf_op jit(solution)/shard_map/ppermute | solution.py:224
  59.0 18.3 %collective-permute-start.12 = (bf16[4,8,16,1024]{3,2,1,0:T(8,128)(2,1)}, bf16[4,8,16,1024]{3,2,1,0:T(8,128)(2,1)S(1)}, u32[]{:S(2)}, u32[]{:S(2)}) collective-permute-start(bf16[4,8,16,1024]{3,2,1,0:T(8,128)(2,1)} %get-tuple-element.28), channel_id=1, source_target_pairs={{0,1},{1,0},{2,3},{3,2},{4,5},{5,4},{6,7},{7,6},{8,9},{9,8},{10,11... | collective-permute-start | bytes 3145736 | tf_op jit(solution)/shard_map/ppermute | solution.py:224
  59.3 11.8 %collective-permute-start.6 = (bf16[256,256]{1,0:T(8,128)(2,1)S(1)}, bf16[256,256]{1,0:T(8,128)(2,1)S(1)}, u32[]{:S(2)}, u32[]{:S(2)}) collective-permute-start(bf16[256,256]{1,0:T(8,128)(2,1)S(1)} %get-tuple-element.41), channel_id=1, source_target_pairs={{0,64},{64,128},{128,192},{192,0},{1,65},{65,129},{129,193},{193,1... | collective-permute-start | bytes 393224 | tf_op jit(solution)/shard_map/ppermute | solution.py:197
  60.6 10.9 %collective-permute-start.8 = (bf16[256,256]{1,0:T(8,128)(2,1)S(1)}, bf16[256,256]{1,0:T(8,128)(2,1)S(1)}, u32[]{:S(2)}, u32[]{:S(2)}) collective-permute-start(bf16[256,256]{1,0:T(8,128)(2,1)S(1)} %get-tuple-element.42), channel_id=1, source_target_pairs={{0,192},{64,0},{128,64},{192,128},{1,193},{65,1},{129,65},{193,129... | collective-permute-start | bytes 393224 | tf_op jit(solution)/shard_map/ppermute | solution.py:197
  62.1 11.8 %collective-permute-start.7 = (bf16[256,256]{1,0:T(8,128)(2,1)S(1)}, bf16[256,256]{1,0:T(8,128)(2,1)S(1)}, u32[]{:S(2)}, u32[]{:S(2)}) collective-permute-start(bf16[256,256]{1,0:T(8,128)(2,1)S(1)} %get-tuple-element.43), channel_id=1, source_target_pairs={{0,128},{64,192},{128,0},{192,64},{1,129},{65,193},{129,1},{193,65... | collective-permute-start | bytes 393224 | tf_op jit(solution)/shard_map/ppermute | solution.py:197
  71.5 21.1 %collective-permute-start.2 = (bf16[64,1024]{1,0:T(8,128)(2,1)}, bf16[64,1024]{1,0:T(8,128)(2,1)}, u32[]{:S(2)}, u32[]{:S(2)}) collective-permute-start(bf16[64,1024]{1,0:T(8,128)(2,1)} %get-tuple-element.49), channel_id=1, source_target_pairs={{0,192},{64,0},{128,64},{192,128},{1,193},{65,1},{129,65},{193,129... | collective-permute-start | bytes 393224 | tf_op jit(solution)/shard_map/ppermute | solution.py:197
  77.3 10.2 %collective-permute-start.18 = (bf16[8,16,1024]{2,1,0:T(8,128)(2,1)S(1)}, bf16[8,16,1024]{2,1,0:T(8,128)(2,1)S(1)}, u32[]{:S(2)}, u32[]{:S(2)}) collective-permute-start(bf16[8,16,1024]{2,1,0:T(8,128)(2,1)S(1)} %get-tuple-element.36), channel_id=1, source_target_pairs={{0,4},{2,6},{4,0},{6,2},{1,5},{3,7},{5,1},{7,3},{8,12},{10,14},{12... | collective-permute-start | bytes 786440 | tf_op jit(solution)/shard_map/ppermute | solution.py:197
  78.3 14.4 %collective-permute-start.1 = (bf16[64,1024]{1,0:T(8,128)(2,1)}, bf16[64,1024]{1,0:T(8,128)(2,1)S(1)}, u32[]{:S(2)}, u32[]{:S(2)}) collective-permute-start(bf16[64,1024]{1,0:T(8,128)(2,1)} %get-tuple-element.50), channel_id=1, source_target_pairs={{0,128},{64,192},{128,0},{192,64},{1,129},{65,193},{129,1},{193,65... | collective-permute-start | bytes 393224 | tf_op jit(solution)/shard_map/ppermute | solution.py:197
  82.0 13.3 %collective-permute-start.13 = (bf16[8,16,1024]{2,1,0:T(8,128)(2,1)S(1)}, bf16[8,16,1024]{2,1,0:T(8,128)(2,1)}, u32[]{:S(2)}, u32[]{:S(2)}) collective-permute-start(bf16[8,16,1024]{2,1,0:T(8,128)(2,1)S(1)} %get-tuple-element.31), channel_id=1, source_target_pairs={{0,2},{2,4},{4,6},{6,0},{1,3},{3,5},{5,7},{7,1},{8,10},{10,12},{12... | collective-permute-start | bytes 786440 | tf_op jit(solution)/shard_map/ppermute | solution.py:197
  82.0 14.5 %collective-permute-start.15 = (bf16[8,16,1024]{2,1,0:T(8,128)(2,1)S(1)}, bf16[8,16,1024]{2,1,0:T(8,128)(2,1)}, u32[]{:S(2)}, u32[]{:S(2)}) collective-permute-start(bf16[8,16,1024]{2,1,0:T(8,128)(2,1)S(1)} %get-tuple-element.32), channel_id=1, source_target_pairs={{0,6},{2,0},{4,2},{6,4},{1,7},{3,1},{5,3},{7,5},{8,14},{10,8},{12,... | collective-permute-start | bytes 786440 | tf_op jit(solution)/shard_map/ppermute | solution.py:197
  87.5 11.4 %collective-permute-start.14 = (bf16[8,16,1024]{2,1,0:T(8,128)(2,1)S(1)}, bf16[8,16,1024]{2,1,0:T(8,128)(2,1)}, u32[]{:S(2)}, u32[]{:S(2)}) collective-permute-start(bf16[8,16,1024]{2,1,0:T(8,128)(2,1)S(1)} %get-tuple-element.33), channel_id=1, source_target_pairs={{0,4},{2,6},{4,0},{6,2},{1,5},{3,7},{5,1},{7,3},{8,12},{10,14},{12... | collective-permute-start | bytes 786440 | tf_op jit(solution)/shard_map/ppermute | solution.py:197
  89.2 13.8 %all-to-all-start.3 = ((bf16[8,16,1024]{2,1,0:T(8,128)(2,1)}), bf16[8,16,1024]{2,1,0:T(8,128)(2,1)S(1)}, u32[]{:S(2)}, u32[]{:S(2)}) async-start(bf16[8,16,1024]{2,1,0:T(8,128)(2,1)} %fusion.2), calls=%async_computation.3 | async-start | bytes 524288 | tf_op jit(solution)/shard_map/all_to_all | solution.py:227
  92.6 8.4 %collective-permute-start.11 = (bf16[256,256]{1,0:T(8,128)(2,1)S(1)}, bf16[256,256]{1,0:T(8,128)(2,1)}, u32[]{:S(2)}, u32[]{:S(2)}) collective-permute-start(bf16[256,256]{1,0:T(8,128)(2,1)S(1)} %fusion.14), channel_id=1, source_target_pairs={{0,64},{64,128},{128,192},{192,0},{1,65},{65,129},{129,193},{193,1... | collective-permute-start | bytes 393224 | tf_op jit(solution)/shard_map/ppermute | solution.py:207
  92.7 16.8 %collective-permute-start.10 = (bf16[256,256]{1,0:T(8,128)(2,1)S(1)}, bf16[256,256]{1,0:T(8,128)(2,1)}, u32[]{:S(2)}, u32[]{:S(2)}) collective-permute-start(bf16[256,256]{1,0:T(8,128)(2,1)S(1)} %fusion.14), channel_id=1, source_target_pairs={{0,128},{64,192},{128,0},{192,64},{1,129},{65,193},{129,1},{193,65... | collective-permute-start | bytes 393224 | tf_op jit(solution)/shard_map/ppermute | solution.py:207
  95.3 14.2 %collective-permute-start.9 = (bf16[256,256]{1,0:T(8,128)(2,1)S(1)}, bf16[256,256]{1,0:T(8,128)(2,1)}, u32[]{:S(2)}, u32[]{:S(2)}) collective-permute-start(bf16[256,256]{1,0:T(8,128)(2,1)S(1)} %fusion.14), channel_id=1, source_target_pairs={{0,192},{64,0},{128,64},{192,128},{1,193},{65,1},{129,65},{193,129... | collective-permute-start | bytes 393224 | tf_op jit(solution)/shard_map/ppermute | solution.py:207
  96.6 36.5 %collective-permute-start.5 = (bf16[64,1024]{1,0:T(8,128)(2,1)S(1)}, bf16[64,1024]{1,0:T(8,128)(2,1)S(1)}, u32[]{:S(2)}, u32[]{:S(2)}) collective-permute-start(bf16[64,1024]{1,0:T(8,128)(2,1)S(1)} %fusion.17), channel_id=1, source_target_pairs={{0,64},{64,128},{128,192},{192,0},{1,65},{65,129},{129,193},{193,1... | collective-permute-start | bytes 393224 | tf_op jit(solution)/shard_map/ppermute | solution.py:207
  98.9 34.3 %collective-permute-start.4 = (bf16[64,1024]{1,0:T(8,128)(2,1)S(1)}, bf16[64,1024]{1,0:T(8,128)(2,1)S(1)}, u32[]{:S(2)}, u32[]{:S(2)}) collective-permute-start(bf16[64,1024]{1,0:T(8,128)(2,1)S(1)} %fusion.17), channel_id=1, source_target_pairs={{0,128},{64,192},{128,0},{192,64},{1,129},{65,193},{129,1},{193,65... | collective-permute-start | bytes 393224 | tf_op jit(solution)/shard_map/ppermute | solution.py:207
  101.0 32.1 %collective-permute-start.3 = (bf16[64,1024]{1,0:T(8,128)(2,1)S(1)}, bf16[64,1024]{1,0:T(8,128)(2,1)S(1)}, u32[]{:S(2)}, u32[]{:S(2)}) collective-permute-start(bf16[64,1024]{1,0:T(8,128)(2,1)S(1)} %fusion.17), channel_id=1, source_target_pairs={{0,192},{64,0},{128,64},{192,128},{1,193},{65,1},{129,65},{193,129... | collective-permute-start | bytes 393224 | tf_op jit(solution)/shard_map/ppermute | solution.py:207
  103.0 15.8 %all-to-all-start.2 = ((bf16[8,16,1024]{2,1,0:T(8,128)(2,1)}), bf16[8,16,1024]{2,1,0:T(8,128)(2,1)S(1)}, u32[]{:S(2)}, u32[]{:S(2)}) async-start(bf16[8,16,1024]{2,1,0:T(8,128)(2,1)} %fusion.5), calls=%async_computation.2 | async-start | bytes 524288 | tf_op jit(solution)/shard_map/all_to_all | solution.py:227
  118.8 27.5 %all-to-all-start.1 = ((bf16[64,16,128]{2,1,0:T(8,128)(2,1)}), bf16[64,16,128]{2,1,0:T(8,128)(2,1)S(1)}, u32[]{:S(2)}, u32[]{:S(2)}) async-start(bf16[64,16,128]{2,1,0:T(8,128)(2,1)} %bitcast.3), calls=%async_computation.1 | async-start | bytes 524288 | tf_op jit(solution)/shard_map/all_to_all | solution.py:267
  133.4 15.8 %collective-permute-start.21 = (bf16[2,16,1024]{2,1,0:T(8,128)(2,1)S(1)}, bf16[2,16,1024]{2,1,0:T(8,128)(2,1)S(1)}, u32[]{:S(2)}, u32[]{:S(2)}) collective-permute-start(bf16[2,16,1024]{2,1,0:T(8,128)(2,1)S(1)} %pad_maximum_fusion.2), channel_id=1, source_target_pairs={{0,64},{64,128},{128,192},{192,0},{1,65},{65,129},{129,193},{193,1... | collective-permute-start | bytes 196616 | tf_op jit(solution)/shard_map/ppermute | solution.py:219
  133.5 15.7 %collective-permute-start.20 = (bf16[2,16,1024]{2,1,0:T(8,128)(2,1)S(1)}, bf16[2,16,1024]{2,1,0:T(8,128)(2,1)S(1)}, u32[]{:S(2)}, u32[]{:S(2)}) collective-permute-start(bf16[2,16,1024]{2,1,0:T(8,128)(2,1)S(1)} %pad_maximum_fusion.2), channel_id=1, source_target_pairs={{0,128},{64,192},{128,0},{192,64},{1,129},{65,193},{129,1},{193,65... | collective-permute-start | bytes 196616 | tf_op jit(solution)/shard_map/ppermute | solution.py:219
  134.4 14.8 %collective-permute-start.22 = (bf16[2,16,1024]{2,1,0:T(8,128)(2,1)S(1)}, bf16[2,16,1024]{2,1,0:T(8,128)(2,1)S(1)}, u32[]{:S(2)}, u32[]{:S(2)}) collective-permute-start(bf16[2,16,1024]{2,1,0:T(8,128)(2,1)S(1)} %pad_maximum_fusion.2), channel_id=1, source_target_pairs={{0,192},{64,0},{128,64},{192,128},{1,193},{65,1},{129,65},{193,129... | collective-permute-start | bytes 196616 | tf_op jit(solution)/shard_map/ppermute | solution.py:219
  (9 other events, 51.7 us)

commit v2 on v1

v2 whole, which is shorter than its diff:
```python
import functools

import jax
import jax.numpy as jnp
from jax import lax
from jax.experimental import pallas as pl
from jax.experimental.pallas import tpu as pltpu
from jax.sharding import Mesh, PartitionSpec as P

ZS, YS, CS = 8, 4, 2
CH = 128
STRIDE = 16
CAP = 12
TILE = 256
BF = jnp.bfloat16
F32 = jnp.float32
ROWS_DIMS = (((0,), (0,)), ((), ()))
COLS_DIMS = (((1,), (1,)), ((), ()))


def dot(a, b):
    return jnp.dot(a, b, preferred_element_type=F32)


def dot_rows(a, b):
    return lax.dot_general(a, b, ROWS_DIMS, preferred_element_type=F32)


def dot_cols(a, b):
    return lax.dot_general(a, b, COLS_DIMS, preferred_element_type=F32)


def iota(shape, dim):
    return lax.broadcasted_iota(jnp.int32, shape, dim)


def pack_kernel(owner_ref, block_ref, spikes_ref, packed_ref, target_ref):
    rows = spikes_ref.shape[0]
    slots = packed_ref.shape[0]
    owners = slots // STRIDE
    owner = owner_ref[...]
    match = owner == iota((owners, rows), 0)
    match_b = match.astype(F32).astype(BF)
    earlier = (iota((rows, rows), 0) < iota((rows, rows), 1)).astype(F32).astype(BF)
    before = dot(match_b, earlier)
    rank = jnp.sum(jnp.where(match, before, 0.0), axis=0, keepdims=True).astype(jnp.int32)
    target = owner * STRIDE + rank
    target_ref[...] = target
    label = (block_ref[...].reshape(1, rows) + 1).astype(F32)
    ranked = jnp.where(iota((CH, rows), 0) == rank, label, 0.0).astype(BF)
    labels = dot_cols(match_b, ranked).astype(BF)
    place = (iota((slots, rows), 0) == target).astype(F32).astype(BF)
    label_place = (iota((slots, owners), 0) == iota((slots, owners), 1) * STRIDE + CAP).astype(F32).astype(BF)
    packed_ref[...] = (dot(place, spikes_ref[...]) + dot(label_place, labels)).astype(BF)


def unpack_kernel(target_ref, back_ref, rebuilt_ref):
    rows = rebuilt_ref.shape[0]
    slots = back_ref.shape[0]
    place = (iota((slots, rows), 0) == target_ref[...]).astype(F32).astype(BF)
    rebuilt_ref[...] = dot_rows(place, back_ref[...]).astype(BF)


def split_pair(core, tile, send_ref, own_ref, at):
    cols = tile.shape[1]
    first = core == 0
    for j in range(8):
        low, high = tile[32 * j : 32 * j + 16], tile[32 * j + 16 : 32 * j + 32]
        z, y = at * 2 + j // 4, j % 4
        send_ref[y, z] = jnp.where(first, high, low).astype(BF)
        own_ref[y, z] = jnp.where(first, low, high).astype(BF)


def forward_kernel(weight, core_ref, count_ref, got_ref, win_hbm, wout_hbm, one_hbm, two_hbm,
                   slots_ref, gout_ref, spread_ref, factors_ref, slope_ref, dlat_ref, send_ref, own_ref,
                   act_ref, lat_ref, err_ref, lab_ref, reb_ref, win_ref, wout_ref, one_ref, two_ref, sems):
    weights = [
        pltpu.make_async_copy(far, near, sems.at[i])
        for i, (far, near) in enumerate(
            [(win_hbm, win_ref), (one_hbm, one_ref), (two_hbm, two_ref), (wout_hbm, wout_ref)]
        )
    ]
    for copy in weights:
        copy.start()
    rows = spread_ref.shape[0]
    per, wide = 16 * CAP, 16 * STRIDE
    row, col = iota((per, wide), 0), iota((per, wide), 1)
    source = (row * 5462) >> 16
    pick = (col == source * STRIDE + row - source * CAP).astype(F32).astype(BF)
    pick_label = (col == source * STRIDE + CAP).astype(F32).astype(BF)
    row1, lane = iota((per, CH), 0), iota((per, CH), 1)
    rank1 = row1 - ((row1 * 5462) >> 16) * CAP
    for b in range(rows // per):
        block = got_ref[b * wide : (b + 1) * wide]
        taken = dot(pick, block)
        label = jnp.sum(jnp.where(lane == rank1, dot(pick_label, block), 0.0), axis=1, keepdims=True)
        counts = jnp.where(label == 1.0, count_ref[0], jnp.where(label == 2.0, count_ref[1], 0))
        inputs = jnp.where(lane < counts, taken, 0.0)
        here = pl.ds(b * per, per)
        lab_ref[here] = label
        spread_ref[here, :CH] = jnp.where(label == 1.0, inputs, 0.0).astype(BF)
        spread_ref[here, CH:] = jnp.where(label == 2.0, inputs, 0.0).astype(BF)

    def step(t):
        here = pl.ds(t * TILE, TILE)
        spread = spread_ref[here]
        if t == 0:
            weights[0].wait()
        factors = dot(spread, win_ref[...]).astype(BF)
        factors_ref[here] = factors
        if t == 0:
            weights[1].wait()
        pre = dot(factors, one_ref[...])
        s = 0.5 * jnp.tanh(0.5 * pre) + 0.5
        silu = pre * s
        slope_ref[here] = (s + silu * (1.0 - s)).astype(BF)
        act = silu.astype(BF)
        act_ref[here] = act
        if t == 0:
            weights[2].wait()
        lat = dot(act, two_ref[...]).astype(BF)
        lat_ref[here] = lat
        if t == 0:
            weights[3].wait()
        both = dot(lat, wout_ref[...])
        label = lab_ref[here]
        is0, is1 = label == 1.0, label == 2.0
        counts = jnp.where(is0, count_ref[0], jnp.where(is1, count_ref[1], 0))
        visible = iota((TILE, CH), 1) < counts
        rates = jnp.where(is0, both[:, :CH], both[:, CH:])
        rates = jnp.where(visible, rates, 0.0)
        reb_ref[here] = rates.astype(BF)
        inputs = spread[:, :CH].astype(F32) + spread[:, CH:].astype(F32)
        errors = ((rates - inputs) * weight)
        err = jnp.concatenate([jnp.where(is0, errors, 0.0), jnp.where(is1, errors, 0.0)], axis=1).astype(BF)
        err_ref[here] = err
        dlat_ref[here] = dot_cols(err, wout_ref[...]).astype(BF)

    for t in range(rows // TILE):
        step(t)
    core = core_ref[0]

    def grads(m, carry):
        cols = pl.ds(pl.multiple_of(m * TILE, TILE), TILE)
        gout = dot_rows(lat_ref[:, cols], err_ref[...]).astype(BF)
        for q in range(4):
            gout_ref[m, :, TILE * q : TILE * q + TILE] = gout[64 * q : 64 * q + 64]
        split_pair(core, dot_rows(act_ref[:, cols], dlat_ref[...]), send_ref, own_ref, m)
        return carry

    lax.fori_loop(0, 4, grads, 0)
    for b in range(rows // per):
        slots_ref[b * wide : (b + 1) * wide] = dot_rows(pick, reb_ref[b * per : (b + 1) * per]).astype(BF)


def inner_kernel(core_ref, dlat_ref, two_ref, slope_ref, factors_ref, dpre_ref, send_ref, own_ref):
    rows = dpre_ref.shape[0]

    def step(t, carry):
        here = pl.ds(pl.multiple_of(t * TILE, TILE), TILE)
        dact = dot_cols(dlat_ref[here], two_ref[...])
        dpre_ref[here] = (dact * slope_ref[here].astype(F32)).astype(BF)
        return carry

    lax.fori_loop(0, rows // TILE, step, 0)
    core = core_ref[0]

    def grads(m, carry):
        cols = pl.ds(pl.multiple_of(m * TILE, TILE), TILE)
        split_pair(core, dot_rows(factors_ref[:, cols], dpre_ref[...]), send_ref, own_ref, m)
        return carry

    lax.fori_loop(0, 4, grads, 0)


def readin_kernel(group_ref, dpre_ref, one_ref, spread_ref, gout_ref, *refs):
    out_refs, dfac_ref, gin_ref = refs[:4], refs[4], refs[5]
    rows = dpre_ref.shape[0]
    for t in range(rows // TILE):
        here = pl.ds(t * TILE, TILE)
        dfac_ref[here] = dot_cols(dpre_ref[here], one_ref[...]).astype(BF)
    grad = dot_rows(spread_ref[...], dfac_ref[...]).astype(BF)
    for j in range(4):
        gin_ref[j] = grad[64 * j : 64 * j + 64]
    for k in range(4):
        at = lax.rem(group_ref[0] + k, 4)
        out_refs[k][:64] = gin_ref[at]
        out_refs[k][64:] = gout_ref[at]


def spread_kernel(group_ref, *refs):
    shares, in_ref, out_ref = refs[:4], refs[4], refs[5]
    for k in range(4):
        at = lax.rem(group_ref[0] + 4 - k, 4)
        in_ref[at] = shares[k][:64].astype(F32)
        for q in range(4):
            out_ref[at, 64 * q : 64 * q + 64] = shares[k][64:, TILE * q : TILE * q + TILE].astype(F32)


def pair_sum_kernel(y_ref, own_ref, got_ref, *out_refs):
    for k, out_ref in enumerate(out_refs):
        at = lax.rem(y_ref[0] + k, YS)
        out_ref[...] = (own_ref[at].astype(F32) + got_ref[at].astype(F32)).astype(BF)


def plane_sum_kernel(*refs):
    out_ref = refs[-1]
    for g in range(2):
        a, b, c, d = [r[...].astype(F32) for r in refs[4 * g : 4 * g + 4]]
        out_ref[:, 16 * g : 16 * g + 16] = ((a + b) + (c + d)).astype(BF)


VM = pl.BlockSpec(memory_space=pltpu.VMEM)
SM = pl.BlockSpec(memory_space=pltpu.SMEM)
FAR = pl.BlockSpec(memory_space=pltpu.HBM)


def call(kernel, outs, *args, smem=0, scratch=(), flops=0, moved=0, vmem=16, far=0):
    return pl.pallas_call(
        kernel,
        out_shape=[jax.ShapeDtypeStruct(s, d) for s, d in outs],
        in_specs=[SM] * smem + [VM] * (len(args) - smem - far) + [FAR] * far,
        out_specs=[VM] * len(outs),
        scratch_shapes=[pltpu.VMEM(s, d) for s, d in scratch] + ([pltpu.SemaphoreType.DMA((far,))] if far else []),
        compiler_params=pltpu.CompilerParams(vmem_limit_bytes=vmem * 1024 * 1024),
        cost_estimate=pl.CostEstimate(flops=flops, bytes_accessed=moved, transcendentals=0),
    )(*args)


def ring(n, k):
    return [(i, (i + k) % n) for i in range(n)]


def others(parts, axis):
    n = len(parts)
    return [parts[0]] + [lax.ppermute(parts[k], axis, ring(n, k)) for k in range(1, n)]


def add_all(terms):
    a, b, c, d = [t.astype(F32) for t in terms]
    return (a + c) + (b + d)


def pair_sum(own, got):
    me = lax.axis_index("y").astype(jnp.int32).reshape(1)
    shape = own.shape[1:]
    return call(pair_sum_kernel, [(shape, BF)] * YS, me, own, got, smem=1, vmem=6, moved=4_000_000)


def gather(x, axis, n):
    me = lax.axis_index(axis)
    got = [x] + [lax.ppermute(x, axis, ring(n, k)) for k in range(1, n)]
    parts = []
    for j in range(n):
        part = got[0]
        for k in range(1, n):
            part = jnp.where((me - k) % n == j, got[k], part)
        parts.append(part)
    return jnp.stack(parts)


def on_device(spikes, row_owner, row_block, chan_count, readin, readout, first_layer, second_layer):
    session = ("z", "y", "core")
    rows = spikes.shape[0]
    owners = ZS * YS * CS
    slots, count = owners * STRIDE, owners * CAP
    lat = readin.shape[1]
    core = lax.axis_index("core").astype(jnp.int32).reshape(1)
    packed, target = call(
        pack_kernel, [((slots, CH), BF), ((1, rows), jnp.int32)],
        row_owner.reshape(1, rows), row_block, spikes, vmem=60,
    )
    got = lax.all_to_all(packed, session, split_axis=0, concat_axis=0, tiled=True)
    weight = (chan_count.shape[0] / rows) ** 0.5
    pair = [((YS, ZS, 16, lat), BF)] * 2
    back, gout, spread, factors, slope, dlat, send2, own2 = call(
        functools.partial(forward_kernel, weight),
        [((slots, CH), BF), ((4, 64, lat), BF), ((count, TILE), BF), ((count, lat), BF), ((count, lat), BF),
         ((count, lat), BF)] + pair,
        core, chan_count, got, readin, readout, first_layer, second_layer,
        smem=2,
        scratch=[((count, lat), BF), ((count, lat), BF), ((count, TILE), BF), ((count, 1), F32), ((count, CH), BF),
                 (readin.shape, BF), (readout.shape, BF), (first_layer.shape, BF), (second_layer.shape, BF)],
        flops=7_000_000_000, moved=16_000_000, vmem=22, far=4,
    )
    dpre, send1, own1 = call(
        inner_kernel, [((count, lat), BF)] + pair, core, dlat, second_layer, slope, factors,
        smem=1, flops=3_200_000_000, moved=12_000_000, vmem=14,
    )
    group = lax.axis_index("group").astype(jnp.int32).reshape(1)
    parts2 = pair_sum(own2, lax.ppermute(send2, "core", ring(CS, 1)))
    parts2, dpre = lax.optimization_barrier((parts2, dpre))
    block_parts = call(
        readin_kernel, [((CH, lat), BF)] * 4, group, dpre, first_layer, spread, gout,
        scratch=[((count, lat), BF), ((4, 64, lat), BF)], smem=1, flops=2_000_000_000, moved=5_000_000, vmem=10,
    )
    terms2 = others(parts2, "y")
    parts1 = pair_sum(own1, lax.ppermute(send1, "core", ring(CS, 1)))
    parts1, block_parts, back = lax.optimization_barrier((parts1, block_parts, back))
    returned = lax.all_to_all(back, session, split_axis=0, concat_axis=0, tiled=True)
    terms1 = others(parts1, "y")
    block_terms = others(block_parts, "group")
    (mine,) = call(plane_sum_kernel, [((ZS, 32, lat), BF)], *terms1, *terms2, vmem=6, moved=6_000_000)
    mine, returned, block_terms = lax.optimization_barrier((mine, returned, block_terms))
    layer_terms = lax.all_to_all(mine, "z", split_axis=0, concat_axis=0, tiled=True)
    share = add_all(block_terms).astype(BF)
    shares = others([share] * 4, "group")
    layer_share = jnp.sum(layer_terms.astype(F32), axis=0).astype(BF)
    scale = 1.0 / (chan_count.shape[0] * owners) ** 0.5
    both = add_all(others([layer_share] * 4, "group")) * scale
    in_sum, out_sum = call(
        spread_kernel, [((4, 64, lat), F32), ((4, TILE, TILE), F32)], group, *shares, smem=1, vmem=10, moved=3_000_000
    )
    (rebuilt,) = call(unpack_kernel, [((rows, CH), BF)], target, returned, vmem=8)
    return rebuilt, in_sum.reshape(TILE, lat), out_sum.reshape(lat, TILE), both[:16], both[16:]


def solution(mesh):
    groups = mesh.shape["group"]
    fine = Mesh(mesh.devices.reshape(groups, ZS, YS, CS), ("group", "z", "y", "core"))
    session = ("z", "y", "core")
    rows = ("group",) + session
    return jax.shard_map(
        on_device,
        mesh=fine,
        in_specs=(P(rows, None), P(rows, None), P(rows), P(session), P(session, None), P(None, session), P(), P()),
        out_specs=(P(rows, None), P(session, None), P(None, session), P(session, None), P(session, None)),
        check_vma=False,
    )
```

time: 151 us -> 129 us (0.85)
  the two profiles are of different devices: /device:TPU:1 before, /device:TPU:6 now
where the time goes in v2:
time: 129 us; the launch traced here: 128 us
  waiting for transfers between devices  44.5 us (34%)
  starting transfers between devices  39.7 us (31%)
  Pallas kernels  28.9 us (22%)
  local copies, waits for them, and re-layouts  12.7 us (10%)
  other arithmetic  1.4 us (1%)
    pallas_call x9, Pallas kernels, call(): pl.pallas_call(kernel, out_shape=[jax.ShapeDtypeStruct(s, d) for s, d in...  28.9 us
    ppermute x15, waiting for transfers between devices, others(): lax.ppermute(parts[k], axis, ring(n, k))  22.6 us
    ppermute x15, starting transfers between devices, others(): lax.ppermute(parts[k], axis, ring(n, k))  18 us
    all_to_all x1, waiting for transfers between devices, on_device(): lax.all_to_all(packed, session, split_axis=0, concat_axis=0, tiled=True)  13 us
    all_to_all x1, starting transfers between devices, on_device(): lax.all_to_all(packed, session, split_axis=0, concat_axis=0, tiled=True)  12.1 us
    unnamed x42, local copies, waits for them, and re-layouts  12.1 us
    all_to_all x1, waiting for transfers between devices, on_device(): lax.all_to_all(mine, 'z', split_axis=0, concat_axis=0, tiled=True)  8.94 us
    all_to_all x1, starting transfers between devices, on_device(): lax.all_to_all(back, session, split_axis=0, concat_axis=0, tiled=True)  5.47 us
  transfers between devices with their start and end apart: 20, of which 8 were waited for; matrix products, arithmetic and copies ran while one was open for 1% of the time, Pallas kernels for 11%

profile of v2, /device:TPU:6, one launch (start us, length us, event | category | flops | bytes accessed | tf_op | source)
XLA Modules:
  0.0 128.1 jit_solution(349017674912076627)
XLA Ops:
  0.6 2.4 %shard_map.119 = (bf16[1024,128]{1,0:T(8,128)(2,1)}, s32[1,384]{1,0:T(1,128)}) custom-call(s32[1,384]{1,0:T(1,128)} %bitcast.14, s32[384]{0:T(512)} %block_ref.1, bf16[384,128]{1,0:T(8,128)(2,1)} %spikes_ref.1), custom_call_target="tpu_custom_call" | custom-call | tf_op jit(solution)/shard_map/pallas_call | solution.py:219
  3.0 12.1 %all-to-all-start = ((bf16[64,16,128]{2,1,0:T(8,128)(2,1)}), bf16[64,16,128]{2,1,0:T(8,128)(2,1)S(1)}, u32[]{:S(2)}, u32[]{:S(2)}) async-start(bf16[64,16,128]{2,1,0:T(8,128)(2,1)} %bitcast.13), calls=%async_computation | async-start | bytes 524288 | tf_op jit(solution)/shard_map/all_to_all | solution.py:273
  15.1 13.0 %all-to-all-done = bf16[64,16,128]{2,1,0:T(8,128)(2,1)S(1)} async-done(((bf16[64,16,128]{2,1,0:T(8,128)(2,1)}), bf16[64,16,128]{2,1,0:T(8,128)(2,1)S(1)}, u32[]{:S(2)}, u32[]{:S(2)}) %all-to-all-start) | async-done | bytes 262176 | tf_op jit(solution)/shard_map/all_to_all | solution.py:273
  28.1 1.6 %copy-done.2 = bf16[1024,1024]{1,0:T(8,128)(2,1)S(1)} copy-done((bf16[1024,1024]{1,0:T(8,128)(2,1)S(1)}, bf16[1024,1024]{1,0:T(8,128)(2,1)}, u32[]{:S(2)}) %copy-start.2) | copy-done | bytes 2097176
  29.7 1.6 %copy-done.3 = bf16[1024,1024]{1,0:T(8,128)(2,1)S(1)} copy-done((bf16[1024,1024]{1,0:T(8,128)(2,1)S(1)}, bf16[1024,1024]{1,0:T(8,128)(2,1)}, u32[]{:S(2)}) %copy-start.3) | copy-done | bytes 2097176
  34.0 11.7 %shard_map.120 = (bf16[1024,128]{1,0:T(8,128)(2,1)S(1)}, bf16[4,64,1024]{2,1,0:T(8,128)(2,1)S(1)}, bf16[768,256]{1,0:T(8,128)(2,1)S(1)}, bf16[768,1024]{1,0:T(8,...) custom-call(s32[1]{0:T(128)} %bitcast.2.core_ref, ...), custom_call_target="tpu_custom_call" | custom-call | flops 7000000000 | bytes 16000000 | tf_op jit(solution)/shard_map/pallas_call | solution.py:219
  46.1 5.7 %shard_map.121 = (bf16[768,1024]{1,0:T(8,128)(2,1)S(1)}, bf16[4,8,16,1024]{3,2,1,0:T(8,128)(2,1)}, bf16[4,8,16,1024]{3,2,1,0:T(8,128)(2,1)S(1)}) custom-call(s32[1]{0:T(128)} %bitcast.2.core_ref, bf16[768,1024]{1,0:T(8,128)(2,1)S(1)} %get-tuple-element.54.dlat_ref, bf16[1024,1024]{1,0:T(8,128)(2,1)S(1)} %copy-done.2, ...), custom_call_target="tpu_custom_call" | custom-call | flops 3200000000 | bytes 12000000 | tf_op jit(solution)/shard_map/pallas_call | solution.py:219
  53.2 2.3 %shard_map.123 = (bf16[8,16,1024]{2,1,0:T(8,128)(2,1)S(1)}, bf16[8,16,1024]{2,1,0:T(8,128)(2,1)}, bf16[8,16,1024]{2,1,0:T(8,128)(2,1)S(1)}, bf16[8,16,1024]{2,1,0:T(8,128)(2,1)S(1)}) custom-call(s32[1]{0:T(128)} %bitcast.1.y_ref, bf16[4,8,16,1024]{3,2,1,0:T(8,128)(2,1)S(1)} %get-tuple-element.63.own_ref, bf16[4,8,16,1024]{3,2,1,0:T(8,128)(2,1)} %collective-permute-done.1.got_ref), custom_call_target="tpu_custom_call" | custom-call | bytes 4000000 | tf_op jit(solution)/shard_map/pallas_call | solution.py:219
  59.8 2.3 %shard_map.124 = (bf16[128,1024]{1,0:T(8,128)(2,1)S(1)}, bf16[128,1024]{1,0:T(8,128)(2,1)S(1)}, bf16[128,1024]{1,0:T(8,128)(2,1)S(1)}, bf16[128,1024]{1,0:T(8,128)(2,1)S(1)}) custom-call(s32[1]{0:T(128)} %bitcast.5.group_ref, bf16[768,1024]{1,0:T(8,128)(2,1)S(1)} %copy-done.14, bf16[1024,1024]{1,0:T(8,128)(2,1)S(1)} %copy-done.4, ...), custom_call_target="tpu_custom_call" | custom-call | flops 2000000000 | bytes 5000000 | tf_op jit(solution)/shard_map/pallas_call | solution.py:219
  64.6 2.4 %collective-permute-start.3 = (bf16[8,16,1024]{2,1,0:T(8,128)(2,1)}, bf16[8,16,1024]{2,1,0:T(8,128)(2,1)S(1)}, u32[]{:S(2)}, u32[]{:S(2)}) collective-permute-start(bf16[8,16,1024]{2,1,0:T(8,128)(2,1)} %get-tuple-element.80), channel_id=1, source_target_pairs={{0,4},{2,6},{4,0},{6,2},{1,5},{3,7},{5,1},{7,3},{8,12},{10,14},{12... | collective-permute-start | bytes 786440 | tf_op jit(solution)/shard_map/ppermute | solution.py:236
  67.1 1.4 %collective-permute-start.4 = (bf16[8,16,1024]{2,1,0:T(8,128)(2,1)}, bf16[8,16,1024]{2,1,0:T(8,128)(2,1)S(1)}, u32[]{:S(2)}, u32[]{:S(2)}) collective-permute-start(bf16[8,16,1024]{2,1,0:T(8,128)(2,1)} %get-tuple-element.81), channel_id=1, source_target_pairs={{0,6},{2,0},{4,2},{6,4},{1,7},{3,1},{5,3},{7,5},{8,14},{10,8},{12,... | collective-permute-start | bytes 786440 | tf_op jit(solution)/shard_map/ppermute | solution.py:236
  69.1 5.5 %all-to-all-start.1 = ((bf16[64,16,128]{2,1,0:T(8,128)(2,1)}), bf16[64,16,128]{2,1,0:T(8,128)(2,1)S(1)}, u32[]{:S(2)}, u32[]{:S(2)}) async-start(bf16[64,16,128]{2,1,0:T(8,128)(2,1)} %bitcast.11), calls=%async_computation.1 | async-start | bytes 524288 | tf_op jit(solution)/shard_map/all_to_all | solution.py:300
  74.6 3.2 %collective-permute-start.6 = (bf16[8,16,1024]{2,1,0:T(8,128)(2,1)}, bf16[8,16,1024]{2,1,0:T(8,128)(2,1)S(1)}, u32[]{:S(2)}, u32[]{:S(2)}) collective-permute-start(bf16[8,16,1024]{2,1,0:T(8,128)(2,1)} %copy-done.11), channel_id=1, source_target_pairs={{0,4},{2,6},{4,0},{6,2},{1,5},{3,7},{5,1},{7,3},{8,12},{10,14},{12... | collective-permute-start | bytes 786440 | tf_op jit(solution)/shard_map/ppermute | solution.py:236
  77.7 2.3 %collective-permute-done.2.refs_1_ = bf16[8,16,1024]{2,1,0:T(8,128)(2,1)S(1)} collective-permute-done((bf16[8,16,1024]{2,1,0:T(8,128)(2,1)}, bf16[8,16,1024]{2,1,0:T(8,128)(2,1)S(1)}, u32[]{:S(2)}, u32[]{:S(2)}) %collective-permute-start.2) | collective-permute-done | bytes 262176 | tf_op jit(solution)/shard_map/ppermute | solution.py:236
  81.0 1.6 %collective-permute-done.4.refs_3_ = bf16[8,16,1024]{2,1,0:T(8,128)(2,1)S(1)} collective-permute-done((bf16[8,16,1024]{2,1,0:T(8,128)(2,1)}, bf16[8,16,1024]{2,1,0:T(8,128)(2,1)S(1)}, u32[]{:S(2)}, u32[]{:S(2)}) %collective-permute-start.4) | collective-permute-done | bytes 262176 | tf_op jit(solution)/shard_map/ppermute | solution.py:236
  83.4 9.8 %collective-permute-done.5.refs_5_ = bf16[8,16,1024]{2,1,0:T(8,128)(2,1)S(1)} collective-permute-done((bf16[8,16,1024]{2,1,0:T(8,128)(2,1)}, bf16[8,16,1024]{2,1,0:T(8,128)(2,1)S(1)}, u32[]{:S(2)}, u32[]{:S(2)}) %collective-permute-start.5) | collective-permute-done | bytes 262176 | tf_op jit(solution)/shard_map/ppermute | solution.py:236
  95.8 5.7 %collective-permute-done.9 = bf16[128,1024]{1,0:T(8,128)(2,1)} collective-permute-done((bf16[128,1024]{1,0:T(8,128)(2,1)}, bf16[128,1024]{1,0:T(8,128)(2,1)}, u32[]{:S(2)}, u32[]{:S(2)}) %collective-permute-start.9) | collective-permute-done | bytes 262176 | tf_op jit(solution)/shard_map/ppermute | solution.py:236
  101.5 3.5 %all-to-all-start.2 = ((bf16[8,32,1024]{2,1,0:T(8,128)(2,1)}), bf16[8,32,1024]{2,1,0:T(8,128)(2,1)S(1)}, u32[]{:S(2)}, u32[]{:S(2)}) async-start(bf16[8,32,1024]{2,1,0:T(8,128)(2,1)} %shard_map.125), calls=%async_computation.2 | async-start | bytes 1048576 | tf_op jit(solution)/shard_map/all_to_all | solution.py:305
  106.8 2.4 %collective-permute-start.12 = (bf16[128,1024]{1,0:T(8,128)(2,1)S(1)}, bf16[128,1024]{1,0:T(8,128)(2,1)S(1)}, u32[]{:S(2)}, u32[]{:S(2)}) collective-permute-start(bf16[128,1024]{1,0:T(8,128)(2,1)S(1)} %add_convert_fusion.refs_0_), channel_id=1, source_target_pairs={{0,128},{64,192},{128,0},{192,64},{1,129},{65,193},{129,1},{193,65... | collective-permute-start | bytes 786440 | tf_op jit(solution)/shard_map/ppermute | solution.py:236
  109.3 8.9 %all-to-all-done.2 = bf16[8,32,1024]{2,1,0:T(8,128)(2,1)S(1)} async-done(((bf16[8,32,1024]{2,1,0:T(8,128)(2,1)}), bf16[8,32,1024]{2,1,0:T(8,128)(2,1)S(1)}, u32[]{:S(2)}, u32[]{:S(2)}) %all-to-all-start.2) | async-done | bytes 524320 | tf_op jit(solution)/shard_map/all_to_all | solution.py:305
  118.3 1.5 %collective-permute-start.14 = (bf16[32,1024]{1,0:T(8,128)(2,1)S(1)}, bf16[32,1024]{1,0:T(8,128)(2,1)S(1)}, u32[]{:S(2)}, u32[]{:S(2)}) collective-permute-start(bf16[32,1024]{1,0:T(8,128)(2,1)S(1)} %reduce_sum.12), channel_id=1, source_target_pairs={{0,128},{64,192},{128,0},{192,64},{1,129},{65,193},{129,1},{193,65... | collective-permute-start | bytes 196616 | tf_op jit(solution)/shard_map/ppermute | solution.py:236
  119.8 2.1 %collective-permute-start.15 = (bf16[32,1024]{1,0:T(8,128)(2,1)S(1)}, bf16[32,1024]{1,0:T(8,128)(2,1)S(1)}, u32[]{:S(2)}, u32[]{:S(2)}) collective-permute-start(bf16[32,1024]{1,0:T(8,128)(2,1)S(1)} %reduce_sum.12), channel_id=1, source_target_pairs={{0,64},{64,128},{128,192},{192,0},{1,65},{65,129},{129,193},{193,1... | collective-permute-start | bytes 196616 | tf_op jit(solution)/shard_map/ppermute | solution.py:236
  123.0 1.4 %shard_map.127 = (f32[4,64,1024]{2,1,0:T(8,128)}, f32[4,256,256]{2,1,0:T(8,128)}) custom-call(s32[1]{0:T(128)} %bitcast.5.group_ref, bf16[128,1024]{1,0:T(8,128)(2,1)S(1)} %add_convert_fusion.refs_0_, bf16[128,1024]{1,0:T(8,128)(2,1)S(1)} %collective-permute-done.11.refs_1_, bf16[128,1024]{1,0:T(8,128)(2,1)S(1)} %collective-permute-done.12.refs_2_, ...), custom_call_target="tpu_custom_call" | custom-call | bytes 3000000 | tf_op jit(solution)/shard_map/pallas_call | solution.py:219
  124.4 2.9 %collective-permute-done.16 = bf16[32,1024]{1,0:T(8,128)(2,1)S(1)} collective-permute-done((bf16[32,1024]{1,0:T(8,128)(2,1)S(1)}, bf16[32,1024]{1,0:T(8,128)(2,1)S(1)}, u32[]{:S(2)}, u32[]{:S(2)}) %collective-permute-start.16) | collective-permute-done | bytes 65568 | tf_op jit(solution)/shard_map/ppermute | solution.py:236
  (71 shorter events, 19.9 us)
Async XLA Ops:
  3.0 25.1 %all-to-all-start = ((bf16[64,16,128]{2,1,0:T(8,128)(2,1)}), bf16[64,16,128]{2,1,0:T(8,128)(2,1)S(1)}, u32[]{:S(2)}, u32[]{:S(2)}) async-start(bf16[64,16,128]{2,1,0:T(8,128)(2,1)} %bitcast.13), calls=%async_computation | async-start | bytes 524288 | tf_op jit(solution)/shard_map/all_to_all | solution.py:273
  45.7 6.1 %copy-start = (bf16[1024,128]{1,0:T(8,128)(2,1)}, bf16[1024,128]{1,0:T(8,128)(2,1)S(1)}, u32[]{:S(2)}) copy-start(bf16[1024,128]{1,0:T(8,128)(2,1)S(1)} %get-tuple-element.86) | copy-start | bytes 786436
  45.7 6.1 %copy-start.15 = (bf16[4,64,1024]{2,1,0:T(8,128)(2,1)}, bf16[4,64,1024]{2,1,0:T(8,128)(2,1)S(1)}, u32[]{:S(2)}) copy-start(bf16[4,64,1024]{2,1,0:T(8,128)(2,1)S(1)} %get-tuple-element.72.gout_ref) | copy-start | bytes 1572868
  45.7 7.5 %collective-permute-start.1 = (bf16[4,8,16,1024]{3,2,1,0:T(8,128)(2,1)}, bf16[4,8,16,1024]{3,2,1,0:T(8,128)(2,1)}, u32[]{:S(2)}, u32[]{:S(2)}) collective-permute-start(bf16[4,8,16,1024]{3,2,1,0:T(8,128)(2,1)} %get-tuple-element.64), channel_id=1, source_target_pairs={{0,1},{1,0},{2,3},{3,2},{4,5},{5,4},{6,7},{7,6},{8,9},{9,8},{10,11... | collective-permute-start | bytes 3145736 | tf_op jit(solution)/shard_map/ppermute | solution.py:291
  53.0 9.1 %collective-permute-start = (bf16[4,8,16,1024]{3,2,1,0:T(8,128)(2,1)}, bf16[4,8,16,1024]{3,2,1,0:T(8,128)(2,1)S(1)}, u32[]{:S(2)}, u32[]{:S(2)}) collective-permute-start(bf16[4,8,16,1024]{3,2,1,0:T(8,128)(2,1)} %get-tuple-element.58), channel_id=1, source_target_pairs={{0,1},{1,0},{2,3},{3,2},{4,5},{5,4},{6,7},{7,6},{8,9},{9,8},{10,11... | collective-permute-start | bytes 3145736 | tf_op jit(solution)/shard_map/ppermute | solution.py:298
  62.1 6.5 %copy-start.8 = (bf16[128,1024]{1,0:T(8,128)(2,1)}, bf16[128,1024]{1,0:T(8,128)(2,1)S(1)}, u32[]{:S(2)}) copy-start(bf16[128,1024]{1,0:T(8,128)(2,1)S(1)} %get-tuple-element.88) | copy-start | bytes 786436
  63.8 16.2 %collective-permute-start.2 = (bf16[8,16,1024]{2,1,0:T(8,128)(2,1)}, bf16[8,16,1024]{2,1,0:T(8,128)(2,1)S(1)}, u32[]{:S(2)}, u32[]{:S(2)}) collective-permute-start(bf16[8,16,1024]{2,1,0:T(8,128)(2,1)} %get-tuple-element.79), channel_id=1, source_target_pairs={{0,2},{2,4},{4,6},{6,0},{1,3},{3,5},{5,7},{7,1},{8,10},{10,12},{12... | collective-permute-start | bytes 786440 | tf_op jit(solution)/shard_map/ppermute | solution.py:236
  64.6 15.6 %collective-permute-start.3 = (bf16[8,16,1024]{2,1,0:T(8,128)(2,1)}, bf16[8,16,1024]{2,1,0:T(8,128)(2,1)S(1)}, u32[]{:S(2)}, u32[]{:S(2)}) collective-permute-start(bf16[8,16,1024]{2,1,0:T(8,128)(2,1)} %get-tuple-element.80), channel_id=1, source_target_pairs={{0,4},{2,6},{4,0},{6,2},{1,5},{3,7},{5,1},{7,3},{8,12},{10,14},{12... | collective-permute-start | bytes 786440 | tf_op jit(solution)/shard_map/ppermute | solution.py:236
  67.1 15.6 %collective-permute-start.4 = (bf16[8,16,1024]{2,1,0:T(8,128)(2,1)}, bf16[8,16,1024]{2,1,0:T(8,128)(2,1)S(1)}, u32[]{:S(2)}, u32[]{:S(2)}) collective-permute-start(bf16[8,16,1024]{2,1,0:T(8,128)(2,1)} %get-tuple-element.81), channel_id=1, source_target_pairs={{0,6},{2,0},{4,2},{6,4},{1,7},{3,1},{5,3},{7,5},{8,14},{10,8},{12,... | collective-permute-start | bytes 786440 | tf_op jit(solution)/shard_map/ppermute | solution.py:236
  68.5 24.8 %collective-permute-start.5 = (bf16[8,16,1024]{2,1,0:T(8,128)(2,1)}, bf16[8,16,1024]{2,1,0:T(8,128)(2,1)S(1)}, u32[]{:S(2)}, u32[]{:S(2)}) collective-permute-start(bf16[8,16,1024]{2,1,0:T(8,128)(2,1)} %get-tuple-element.83), channel_id=1, source_target_pairs={{0,2},{2,4},{4,6},{6,0},{1,3},{3,5},{5,7},{7,1},{8,10},{10,12},{12... | collective-permute-start | bytes 786440 | tf_op jit(solution)/shard_map/ppermute | solution.py:236
  69.1 32.4 %all-to-all-start.1 = ((bf16[64,16,128]{2,1,0:T(8,128)(2,1)}), bf16[64,16,128]{2,1,0:T(8,128)(2,1)S(1)}, u32[]{:S(2)}, u32[]{:S(2)}) async-start(bf16[64,16,128]{2,1,0:T(8,128)(2,1)} %bitcast.11), calls=%async_computation.1 | async-start | bytes 524288 | tf_op jit(solution)/shard_map/all_to_all | solution.py:300
  74.6 20.1 %collective-permute-start.6 = (bf16[8,16,1024]{2,1,0:T(8,128)(2,1)}, bf16[8,16,1024]{2,1,0:T(8,128)(2,1)S(1)}, u32[]{:S(2)}, u32[]{:S(2)}) collective-permute-start(bf16[8,16,1024]{2,1,0:T(8,128)(2,1)} %copy-done.11), channel_id=1, source_target_pairs={{0,4},{2,6},{4,0},{6,2},{1,5},{3,7},{5,1},{7,3},{8,12},{10,14},{12... | collective-permute-start | bytes 786440 | tf_op jit(solution)/shard_map/ppermute | solution.py:236
  80.0 14.7 %collective-permute-start.7 = (bf16[8,16,1024]{2,1,0:T(8,128)(2,1)}, bf16[8,16,1024]{2,1,0:T(8,128)(2,1)S(1)}, u32[]{:S(2)}, u32[]{:S(2)}) collective-permute-start(bf16[8,16,1024]{2,1,0:T(8,128)(2,1)} %copy-done.10), channel_id=1, source_target_pairs={{0,6},{2,0},{4,2},{6,4},{1,7},{3,1},{5,3},{7,5},{8,14},{10,8},{12,... | collective-permute-start | bytes 786440 | tf_op jit(solution)/shard_map/ppermute | solution.py:236
  80.2 15.6 %collective-permute-start.10 = (bf16[128,1024]{1,0:T(8,128)(2,1)}, bf16[128,1024]{1,0:T(8,128)(2,1)S(1)}, u32[]{:S(2)}, u32[]{:S(2)}) collective-permute-start(bf16[128,1024]{1,0:T(8,128)(2,1)} %copy-done.9), channel_id=1, source_target_pairs={{0,192},{64,0},{128,64},{192,128},{1,193},{65,1},{129,65},{193,129... | collective-permute-start | bytes 786440 | tf_op jit(solution)/shard_map/ppermute | solution.py:236
  82.7 13.1 %collective-permute-start.8 = (bf16[128,1024]{1,0:T(8,128)(2,1)}, bf16[128,1024]{1,0:T(8,128)(2,1)S(1)}, u32[]{:S(2)}, u32[]{:S(2)}) collective-permute-start(bf16[128,1024]{1,0:T(8,128)(2,1)} %copy-done.8), channel_id=1, source_target_pairs={{0,64},{64,128},{128,192},{192,0},{1,65},{65,129},{129,193},{193,1... | collective-permute-start | bytes 786440 | tf_op jit(solution)/shard_map/ppermute | solution.py:236
  93.3 8.2 %collective-permute-start.9 = (bf16[128,1024]{1,0:T(8,128)(2,1)}, bf16[128,1024]{1,0:T(8,128)(2,1)}, u32[]{:S(2)}, u32[]{:S(2)}) collective-permute-start(bf16[128,1024]{1,0:T(8,128)(2,1)} %copy-done.7), channel_id=1, source_target_pairs={{0,128},{64,192},{128,0},{192,64},{1,129},{65,193},{129,1},{193,65... | collective-permute-start | bytes 786440 | tf_op jit(solution)/shard_map/ppermute | solution.py:236
  95.8 26.1 %copy-start.1 = (s32[1,384]{1,0:T(1,128)S(1)}, s32[1,384]{1,0:T(1,128)}, u32[]{:S(2)}) copy-start(s32[1,384]{1,0:T(1,128)} %get-tuple-element.52.target_ref) | copy-start | bytes 4612
  101.5 16.7 %all-to-all-start.2 = ((bf16[8,32,1024]{2,1,0:T(8,128)(2,1)}), bf16[8,32,1024]{2,1,0:T(8,128)(2,1)S(1)}, u32[]{:S(2)}, u32[]{:S(2)}) async-start(bf16[8,32,1024]{2,1,0:T(8,128)(2,1)} %shard_map.125), calls=%async_computation.2 | async-start | bytes 1048576 | tf_op jit(solution)/shard_map/all_to_all | solution.py:305
  106.3 15.6 %collective-permute-start.11 = (bf16[128,1024]{1,0:T(8,128)(2,1)S(1)}, bf16[128,1024]{1,0:T(8,128)(2,1)S(1)}, u32[]{:S(2)}, u32[]{:S(2)}) collective-permute-start(bf16[128,1024]{1,0:T(8,128)(2,1)S(1)} %add_convert_fusion.refs_0_), channel_id=1, source_target_pairs={{0,64},{64,128},{128,192},{192,0},{1,65},{65,129},{129,193},{193,1... | collective-permute-start | bytes 786440 | tf_op jit(solution)/shard_map/ppermute | solution.py:236
  106.8 16.1 %collective-permute-start.12 = (bf16[128,1024]{1,0:T(8,128)(2,1)S(1)}, bf16[128,1024]{1,0:T(8,128)(2,1)S(1)}, u32[]{:S(2)}, u32[]{:S(2)}) collective-permute-start(bf16[128,1024]{1,0:T(8,128)(2,1)S(1)} %add_convert_fusion.refs_0_), channel_id=1, source_target_pairs={{0,128},{64,192},{128,0},{192,64},{1,129},{65,193},{129,1},{193,65... | collective-permute-start | bytes 786440 | tf_op jit(solution)/shard_map/ppermute | solution.py:236
  109.3 13.7 %collective-permute-start.13 = (bf16[128,1024]{1,0:T(8,128)(2,1)S(1)}, bf16[128,1024]{1,0:T(8,128)(2,1)S(1)}, u32[]{:S(2)}, u32[]{:S(2)}) collective-permute-start(bf16[128,1024]{1,0:T(8,128)(2,1)S(1)} %add_convert_fusion.refs_0_), channel_id=1, source_target_pairs={{0,192},{64,0},{128,64},{192,128},{1,193},{65,1},{129,65},{193,129... | collective-permute-start | bytes 786440 | tf_op jit(solution)/shard_map/ppermute | solution.py:236
  118.3 6.1 %collective-permute-start.14 = (bf16[32,1024]{1,0:T(8,128)(2,1)S(1)}, bf16[32,1024]{1,0:T(8,128)(2,1)S(1)}, u32[]{:S(2)}, u32[]{:S(2)}) collective-permute-start(bf16[32,1024]{1,0:T(8,128)(2,1)S(1)} %reduce_sum.12), channel_id=1, source_target_pairs={{0,128},{64,192},{128,0},{192,64},{1,129},{65,193},{129,1},{193,65... | collective-permute-start | bytes 196616 | tf_op jit(solution)/shard_map/ppermute | solution.py:236
  119.8 4.6 %collective-permute-start.15 = (bf16[32,1024]{1,0:T(8,128)(2,1)S(1)}, bf16[32,1024]{1,0:T(8,128)(2,1)S(1)}, u32[]{:S(2)}, u32[]{:S(2)}) collective-permute-start(bf16[32,1024]{1,0:T(8,128)(2,1)S(1)} %reduce_sum.12), channel_id=1, source_target_pairs={{0,64},{64,128},{128,192},{192,0},{1,65},{65,129},{129,193},{193,1... | collective-permute-start | bytes 196616 | tf_op jit(solution)/shard_map/ppermute | solution.py:236
  121.9 5.5 %collective-permute-start.16 = (bf16[32,1024]{1,0:T(8,128)(2,1)S(1)}, bf16[32,1024]{1,0:T(8,128)(2,1)S(1)}, u32[]{:S(2)}, u32[]{:S(2)}) collective-permute-start(bf16[32,1024]{1,0:T(8,128)(2,1)S(1)} %reduce_sum.12), channel_id=1, source_target_pairs={{0,192},{64,0},{128,64},{192,128},{1,193},{65,1},{129,65},{193,129... | collective-permute-start | bytes 196616 | tf_op jit(solution)/shard_map/ppermute | solution.py:236
  (17 other events, 38.4 us)

commit v3 on v2

--- a/solution.py
+++ b/solution.py
@@ -61,25 +61,23 @@
     rebuilt_ref[...] = dot_rows(place, back_ref[...]).astype(BF)
 
 
-def split_pair(core, tile, send_ref, own_ref, at):
-    cols = tile.shape[1]
+def split_pair(core, tile, send_ref, own_ref, at, layer):
+    here = slice(16 * layer, 16 * layer + 16)
     first = core == 0
     for j in range(8):
         low, high = tile[32 * j : 32 * j + 16], tile[32 * j + 16 : 32 * j + 32]
         z, y = at * 2 + j // 4, j % 4
-        send_ref[y, z] = jnp.where(first, high, low).astype(BF)
-        own_ref[y, z] = jnp.where(first, low, high).astype(BF)
-
-
-def forward_kernel(weight, core_ref, count_ref, got_ref, win_hbm, wout_hbm, one_hbm, two_hbm,
-                   slots_ref, gout_ref, spread_ref, factors_ref, slope_ref, dlat_ref, send_ref, own_ref,
-                   act_ref, lat_ref, err_ref, lab_ref, reb_ref, win_ref, wout_ref, one_ref, two_ref, sems):
-    weights = [
-        pltpu.make_async_copy(far, near, sems.at[i])
-        for i, (far, near) in enumerate(
-            [(win_hbm, win_ref), (one_hbm, one_ref), (two_hbm, two_ref), (wout_hbm, wout_ref)]
-        )
-    ]
+        send_ref[y, z, here] = jnp.where(first, high, low).astype(BF)
+        own_ref[y, z, here] = jnp.where(first, low, high).astype(BF)
+
+
+def work_kernel(weight, core_ref, group_ref, count_ref, win_hbm, one_hbm, two_hbm, wout_hbm, got_ref,
+                slots_ref, part0_ref, part1_ref, part2_ref, part3_ref, send_ref, own_ref,
+                win_ref, one_ref, two_ref, wout_ref, spread_ref, factors_ref, slope_ref, act_ref, lat_ref, err_ref,
+                dlat_ref, lab_ref, reb_ref, gout_ref, gin_ref, sems):
+    far = (win_hbm, one_hbm, two_hbm, wout_hbm)
+    near = (win_ref, one_ref, two_ref, wout_ref)
+    weights = [pltpu.make_async_copy(far[i], near[i], sems.at[i]) for i in range(4)]
     for copy in weights:
         copy.start()
     rows = spread_ref.shape[0]
@@ -145,47 +143,34 @@
         gout = dot_rows(lat_ref[:, cols], err_ref[...]).astype(BF)
         for q in range(4):
             gout_ref[m, :, TILE * q : TILE * q + TILE] = gout[64 * q : 64 * q + 64]
-        split_pair(core, dot_rows(act_ref[:, cols], dlat_ref[...]), send_ref, own_ref, m)
+        split_pair(core, dot_rows(act_ref[:, cols], dlat_ref[...]), send_ref, own_ref, m, 1)
         return carry
 
     lax.fori_loop(0, 4, grads, 0)
     for b in range(rows // per):
         slots_ref[b * wide : (b + 1) * wide] = dot_rows(pick, reb_ref[b * per : (b + 1) * per]).astype(BF)
 
-
-def inner_kernel(core_ref, dlat_ref, two_ref, slope_ref, factors_ref, dpre_ref, send_ref, own_ref):
-    rows = dpre_ref.shape[0]
-
-    def step(t, carry):
-        here = pl.ds(pl.multiple_of(t * TILE, TILE), TILE)
-        dact = dot_cols(dlat_ref[here], two_ref[...])
-        dpre_ref[here] = (dact * slope_ref[here].astype(F32)).astype(BF)
-        return carry
-
-    lax.fori_loop(0, rows // TILE, step, 0)
-    core = core_ref[0]
-
-    def grads(m, carry):
-        cols = pl.ds(pl.multiple_of(m * TILE, TILE), TILE)
-        split_pair(core, dot_rows(factors_ref[:, cols], dpre_ref[...]), send_ref, own_ref, m)
-        return carry
-
-    lax.fori_loop(0, 4, grads, 0)
-
-
-def readin_kernel(group_ref, dpre_ref, one_ref, spread_ref, gout_ref, *refs):
-    out_refs, dfac_ref, gin_ref = refs[:4], refs[4], refs[5]
-    rows = dpre_ref.shape[0]
     for t in range(rows // TILE):
         here = pl.ds(t * TILE, TILE)
-        dfac_ref[here] = dot_cols(dpre_ref[here], one_ref[...]).astype(BF)
-    grad = dot_rows(spread_ref[...], dfac_ref[...]).astype(BF)
+        dact = dot_cols(dlat_ref[here], two_ref[...])
+        slope_ref[here] = (dact * slope_ref[here].astype(F32)).astype(BF)
+
+    def first(m, carry):
+        cols = pl.ds(pl.multiple_of(m * TILE, TILE), TILE)
+        split_pair(core, dot_rows(factors_ref[:, cols], slope_ref[...]), send_ref, own_ref, m, 0)
+        return carry
+
+    lax.fori_loop(0, 4, first, 0)
+    for t in range(rows // TILE):
+        here = pl.ds(t * TILE, TILE)
+        dlat_ref[here] = dot_cols(slope_ref[here], one_ref[...]).astype(BF)
+    grad = dot_rows(spread_ref[...], dlat_ref[...]).astype(BF)
     for j in range(4):
         gin_ref[j] = grad[64 * j : 64 * j + 64]
-    for k in range(4):
+    for k, part_ref in enumerate((part0_ref, part1_ref, part2_ref, part3_ref)):
         at = lax.rem(group_ref[0] + k, 4)
-        out_refs[k][:64] = gin_ref[at]
-        out_refs[k][64:] = gout_ref[at]
+        part_ref[:64] = gin_ref[at]
+        part_ref[64:] = gout_ref[at]
 
 
 def spread_kernel(group_ref, *refs):
@@ -203,25 +188,23 @@
         out_ref[...] = (own_ref[at].astype(F32) + got_ref[at].astype(F32)).astype(BF)
 
 
-def plane_sum_kernel(*refs):
-    out_ref = refs[-1]
-    for g in range(2):
-        a, b, c, d = [r[...].astype(F32) for r in refs[4 * g : 4 * g + 4]]
-        out_ref[:, 16 * g : 16 * g + 16] = ((a + b) + (c + d)).astype(BF)
+def plane_sum_kernel(a_ref, b_ref, c_ref, d_ref, out_ref):
+    a, b, c, d = [r[...].astype(F32) for r in (a_ref, b_ref, c_ref, d_ref)]
+    out_ref[...] = ((a + b) + (c + d)).astype(BF)
 
 
 VM = pl.BlockSpec(memory_space=pltpu.VMEM)
 SM = pl.BlockSpec(memory_space=pltpu.SMEM)
-FAR = pl.BlockSpec(memory_space=pltpu.HBM)
+ANY = pl.BlockSpec(memory_space=pl.ANY)
 
 
 def call(kernel, outs, *args, smem=0, scratch=(), flops=0, moved=0, vmem=16, far=0):
     return pl.pallas_call(
         kernel,
         out_shape=[jax.ShapeDtypeStruct(s, d) for s, d in outs],
-        in_specs=[SM] * smem + [VM] * (len(args) - smem - far) + [FAR] * far,
+        in_specs=[SM] * smem + [ANY] * far + [VM] * (len(args) - smem - far),
         out_specs=[VM] * len(outs),
-        scratch_shapes=[pltpu.VMEM(s, d) for s, d in scratch] + ([pltpu.SemaphoreType.DMA((far,))] if far else []),
+        scratch_shapes=[pltpu.VMEM(s, d) for s, d in scratch] + [pltpu.SemaphoreType.DMA((far,))] * (far > 0),
         compiler_params=pltpu.CompilerParams(vmem_limit_bytes=vmem * 1024 * 1024),
         cost_estimate=pl.CostEstimate(flops=flops, bytes_accessed=moved, transcendentals=0),
     )(*args)
@@ -239,24 +222,6 @@
 def add_all(terms):
     a, b, c, d = [t.astype(F32) for t in terms]
     return (a + c) + (b + d)
-
-
-def pair_sum(own, got):
-    me = lax.axis_index("y").astype(jnp.int32).reshape(1)
-    shape = own.shape[1:]
-    return call(pair_sum_kernel, [(shape, BF)] * YS, me, own, got, smem=1, vmem=6, moved=4_000_000)
-
-
-def gather(x, axis, n):
-    me = lax.axis_index(axis)
-    got = [x] + [lax.ppermute(x, axis, ring(n, k)) for k in range(1, n)]
-    parts = []
-    for j in range(n):
-        part = got[0]
-        for k in range(1, n):
-            part = jnp.where((me - k) % n == j, got[k], part)
-        parts.append(part)
-    return jnp.stack(parts)
 
 
 def on_device(spikes, row_owner, row_block, chan_count, readin, readout, first_layer, second_layer):
@@ -272,35 +237,29 @@
     )
     got = lax.all_to_all(packed, session, split_axis=0, concat_axis=0, tiled=True)
     weight = (chan_count.shape[0] / rows) ** 0.5
-    pair = [((YS, ZS, 16, lat), BF)] * 2
-    back, gout, spread, factors, slope, dlat, send2, own2 = call(
-        functools.partial(forward_kernel, weight),
-        [((slots, CH), BF), ((4, 64, lat), BF), ((count, TILE), BF), ((count, lat), BF), ((count, lat), BF),
-         ((count, lat), BF)] + pair,
-        core, chan_count, got, readin, readout, first_layer, second_layer,
-        smem=2,
-        scratch=[((count, lat), BF), ((count, lat), BF), ((count, TILE), BF), ((count, 1), F32), ((count, CH), BF),
-                 (readin.shape, BF), (readout.shape, BF), (first_layer.shape, BF), (second_layer.shape, BF)],
-        flops=7_000_000_000, moved=16_000_000, vmem=22, far=4,
-    )
-    dpre, send1, own1 = call(
-        inner_kernel, [((count, lat), BF)] + pair, core, dlat, second_layer, slope, factors,
-        smem=1, flops=3_200_000_000, moved=12_000_000, vmem=14,
-    )
     group = lax.axis_index("group").astype(jnp.int32).reshape(1)
-    parts2 = pair_sum(own2, lax.ppermute(send2, "core", ring(CS, 1)))
-    parts2, dpre = lax.optimization_barrier((parts2, dpre))
-    block_parts = call(
-        readin_kernel, [((CH, lat), BF)] * 4, group, dpre, first_layer, spread, gout,
-        scratch=[((count, lat), BF), ((4, 64, lat), BF)], smem=1, flops=2_000_000_000, moved=5_000_000, vmem=10,
-    )
-    terms2 = others(parts2, "y")
-    parts1 = pair_sum(own1, lax.ppermute(send1, "core", ring(CS, 1)))
-    parts1, block_parts, back = lax.optimization_barrier((parts1, block_parts, back))
+    pair = ((YS, ZS, 32, lat), BF)
+    tall, narrow = ((count, lat), BF), ((count, TILE), BF)
+    back, *rest = call(
+        functools.partial(work_kernel, weight),
+        [((slots, CH), BF)] + [((CH, lat), BF)] * 4 + [pair, pair],
+        core, group, chan_count, readin, first_layer, second_layer, readout, got,
+        smem=3, far=4,
+        scratch=[(readin.shape, BF), (first_layer.shape, BF), (second_layer.shape, BF), (readout.shape, BF),
+                 narrow, tall, tall, tall, tall, narrow, tall, ((count, 1), F32), ((count, CH), BF),
+                 ((4, 64, lat), BF), ((4, 64, lat), BF)],
+        flops=12_000_000_000, moved=12_000_000, vmem=58,
+    )
+    block_parts, (send, own) = rest[:4], rest[4:]
+    y_at = lax.axis_index("y").astype(jnp.int32).reshape(1)
+    parts = call(
+        pair_sum_kernel, [((ZS, 32, lat), BF)] * YS, y_at, own, lax.ppermute(send, "core", ring(CS, 1)),
+        smem=1, vmem=10, moved=8_000_000,
+    )
+    parts, block_parts, back = lax.optimization_barrier((parts, block_parts, back))
     returned = lax.all_to_all(back, session, split_axis=0, concat_axis=0, tiled=True)
-    terms1 = others(parts1, "y")
     block_terms = others(block_parts, "group")
-    (mine,) = call(plane_sum_kernel, [((ZS, 32, lat), BF)], *terms1, *terms2, vmem=6, moved=6_000_000)
+    (mine,) = call(plane_sum_kernel, [((ZS, 32, lat), BF)], *others(parts, "y"), vmem=6, moved=3_000_000)
     mine, returned, block_terms = lax.optimization_barrier((mine, returned, block_terms))
     layer_terms = lax.all_to_all(mine, "z", split_axis=0, concat_axis=0, tiled=True)
     share = add_all(block_terms).astype(BF)

time: 129 us -> 122 us (0.946)
  local copies, waits for them, and re-layouts: 12.7 us -> 3.66 us
  waiting for transfers between devices: 44.5 us -> 52.6 us
  starting transfers between devices: 39.7 us -> 37 us
  Pallas kernels: 28.9 us -> 26.8 us
    unnamed x42 -> x10, local copies, waits for them, and re-layouts: 12.1 us -> 3 us
    ppermute x2 -> x1, waiting for transfers between devices: 0.01 us -> 4.13 us  [on_device(): lax.ppermute(send, 'core', ring(CS, 1))]
    ppermute x15 -> x12, starting transfers between devices: 18 us -> 15.1 us  [others(): lax.ppermute(parts[k], axis, ring(n, k))]
    all_to_all x1, waiting for transfers between devices: 8.94 us -> 11.2 us  [on_device(): lax.all_to_all(mine, 'z', split_axis=0, concat_axis=0, tiled=True)]
    pallas_call x9 -> x6, Pallas kernels: 28.9 us -> 26.8 us  [call(): pl.pallas_call(kernel, out_shape=[jax.ShapeDtypeStruct(s, d) for s, d in...]
    ppermute x15 -> x12, waiting for transfers between devices: 22.6 us -> 24.2 us  [others(): lax.ppermute(parts[k], axis, ring(n, k))]
  transfers between devices with their start and end apart: 20 -> 16, of which waited for: 8 -> 7; matrix products, arithmetic and copies ran while one was open for 1% -> 1% of each run, Pallas kernels for 11% -> 3%
where the time goes in v3:
time: 122 us
  waiting for transfers between devices  52.6 us (43%)
  starting transfers between devices  37 us (30%)
  Pallas kernels  26.8 us (22%)
  local copies, waits for them, and re-layouts  3.66 us (3%)
  other arithmetic  1.32 us (1%)
    pallas_call x6, Pallas kernels, call(): pl.pallas_call(kernel, out_shape=[jax.ShapeDtypeStruct(s, d) for s, d in...  26.8 us
    ppermute x12, waiting for transfers between devices, others(): lax.ppermute(parts[k], axis, ring(n, k))  24.2 us
    ppermute x12, starting transfers between devices, others(): lax.ppermute(parts[k], axis, ring(n, k))  15.1 us
    all_to_all x1, waiting for transfers between devices, on_device(): lax.all_to_all(packed, session, split_axis=0, concat_axis=0, tiled=True)  13 us
    all_to_all x1, starting transfers between devices, on_device(): lax.all_to_all(packed, session, split_axis=0, concat_axis=0, tiled=True)  12.1 us
    all_to_all x1, waiting for transfers between devices, on_device(): lax.all_to_all(mine, 'z', split_axis=0, concat_axis=0, tiled=True)  11.2 us
    all_to_all x1, starting transfers between devices, on_device(): lax.all_to_all(back, session, split_axis=0, concat_axis=0, tiled=True)  5.36 us
    ppermute x1, waiting for transfers between devices, on_device(): lax.ppermute(send, 'core', ring(CS, 1))  4.13 us
  transfers between devices with their start and end apart: 16, of which 7 were waited for; matrix products, arithmetic and copies ran while one was open for 1% of the time, Pallas kernels for 3%

profile of v3, /device:TPU:6, one launch (start us, length us, event | category | flops | bytes accessed | tf_op | source)
XLA Modules:
  0.0 122.0 jit_solution(2506241988066676011)
XLA Ops:
  0.6 2.4 %shard_map.119 = (bf16[1024,128]{1,0:T(8,128)(2,1)}, s32[1,384]{1,0:T(1,128)}) custom-call(s32[1,384]{1,0:T(1,128)} %bitcast.14, s32[384]{0:T(512)} %block_ref.1, bf16[384,128]{1,0:T(8,128)(2,1)} %spikes_ref.1), custom_call_target="tpu_custom_call" | custom-call | tf_op jit(solution)/shard_map/pallas_call | solution.py:202
  3.0 12.1 %all-to-all-start = ((bf16[64,16,128]{2,1,0:T(8,128)(2,1)}), bf16[64,16,128]{2,1,0:T(8,128)(2,1)S(1)}, u32[]{:S(2)}, u32[]{:S(2)}) async-start(bf16[64,16,128]{2,1,0:T(8,128)(2,1)} %bitcast.13), calls=%async_computation | async-start | bytes 524288 | tf_op jit(solution)/shard_map/all_to_all | solution.py:238
  15.1 13.0 %all-to-all-done = bf16[64,16,128]{2,1,0:T(8,128)(2,1)S(1)} async-done(((bf16[64,16,128]{2,1,0:T(8,128)(2,1)}), bf16[64,16,128]{2,1,0:T(8,128)(2,1)S(1)}, u32[]{:S(2)}, u32[]{:S(2)}) %all-to-all-start) | async-done | bytes 262176 | tf_op jit(solution)/shard_map/all_to_all | solution.py:238
  28.8 19.5 %shard_map.120 = (bf16[1024,128]{1,0:T(8,128)(2,1)}, bf16[128,1024]{1,0:T(8,128)(2,1)}, bf16[128,1024]{1,0:T(8,128)(2,1)}, bf16[128,1024]{1,0:T(8,128)(2,1)}, bf...) custom-call(s32[1]{0:T(128)} %bitcast.2.core_ref, s32[1]{0:T(128)} %bitcast.3.group_ref, ...), custom_call_target="tpu_custom_call" | custom-call | flops 12000000000 | bytes 12000000 | tf_op jit(solution)/shard_map/pallas_call | solution.py:202
  48.6 4.1 %collective-permute-done.got_ref = bf16[4,8,32,1024]{3,2,1,0:T(8,128)(2,1)S(1)} collective-permute-done((bf16[4,8,32,1024]{3,2,1,0:T(8,128)(2,1)}, bf16[4,8,32,1024]{3,2,1,0:T(8,128)(2,1)S(1)}, u32[]{:S(2)}, u32[]{:S(2)}) %collective-permute-start) | collective-permute-done | bytes 2097184 | tf_op jit(solution)/shard_map/ppermute | solution.py:256
  52.8 1.6 %copy-done = bf16[4,8,32,1024]{3,2,1,0:T(8,128)(2,1)S(1)} copy-done((bf16[4,8,32,1024]{3,2,1,0:T(8,128)(2,1)S(1)}, bf16[4,8,32,1024]{3,2,1,0:T(8,128)(2,1)}, u32[]{:S(2)}) %copy-start) | copy-done | bytes 2097176
  54.3 1.4 %shard_map.121 = (bf16[8,32,1024]{2,1,0:T(8,128)(2,1)S(1)}, bf16[8,32,1024]{2,1,0:T(8,128)(2,1)}, bf16[8,32,1024]{2,1,0:T(8,128)(2,1)}, bf16[8,32,1024]{2,1,0:T(8,128)(2,1)S(1)}) custom-call(s32[1]{0:T(128)} %bitcast.1.y_ref, bf16[4,8,32,1024]{3,2,1,0:T(8,128)(2,1)S(1)} %copy-done, bf16[4,8,32,1024]{3,2,1,0:T(8,128)(2,1)S(1)} %collective-permute-done.got_ref), custom_call_target="tpu_custom_call" | custom-call | bytes 8000000 | tf_op jit(solution)/shard_map/pallas_call | solution.py:202
  55.7 0.8 collective-permute-start.1
  56.5 2.4 %collective-permute-start.2 = (bf16[8,32,1024]{2,1,0:T(8,128)(2,1)}, bf16[8,32,1024]{2,1,0:T(8,128)(2,1)S(1)}, u32[]{:S(2)}, u32[]{:S(2)}) collective-permute-start(bf16[8,32,1024]{2,1,0:T(8,128)(2,1)} %get-tuple-element.50), channel_id=1, source_target_pairs={{0,4},{2,6},{4,0},{6,2},{1,5},{3,7},{5,1},{7,3},{8,12},{10,14},{12... | collective-permute-start | bytes 1572872 | tf_op jit(solution)/shard_map/ppermute | solution.py:219
  58.9 1.4 %collective-permute-start.3 = (bf16[8,32,1024]{2,1,0:T(8,128)(2,1)S(1)}, bf16[8,32,1024]{2,1,0:T(8,128)(2,1)S(1)}, u32[]{:S(2)}, u32[]{:S(2)}) collective-permute-start(bf16[8,32,1024]{2,1,0:T(8,128)(2,1)S(1)} %get-tuple-element.51), channel_id=1, source_target_pairs={{0,6},{2,0},{4,2},{6,4},{1,7},{3,1},{5,3},{7,5},{8,14},{10,8},{12,... | collective-permute-start | bytes 1572872 | tf_op jit(solution)/shard_map/ppermute | solution.py:219
  60.4 5.4 %all-to-all-start.1 = ((bf16[64,16,128]{2,1,0:T(8,128)(2,1)}), bf16[64,16,128]{2,1,0:T(8,128)(2,1)S(1)}, u32[]{:S(2)}, u32[]{:S(2)}) async-start(bf16[64,16,128]{2,1,0:T(8,128)(2,1)} %bitcast.11), calls=%async_computation.1 | async-start | bytes 524288 | tf_op jit(solution)/shard_map/all_to_all | solution.py:260
  66.3 2.4 %collective-permute-start.5 = (bf16[128,1024]{1,0:T(8,128)(2,1)}, bf16[128,1024]{1,0:T(8,128)(2,1)S(1)}, u32[]{:S(2)}, u32[]{:S(2)}) collective-permute-start(bf16[128,1024]{1,0:T(8,128)(2,1)} %get-tuple-element.55), channel_id=1, source_target_pairs={{0,128},{64,192},{128,0},{192,64},{1,129},{65,193},{129,1},{193,65... | collective-permute-start | bytes 786440 | tf_op jit(solution)/shard_map/ppermute | solution.py:219
  68.7 15.7 %collective-permute-done.1.b_ref = bf16[8,32,1024]{2,1,0:T(8,128)(2,1)S(1)} collective-permute-done((bf16[8,32,1024]{2,1,0:T(8,128)(2,1)}, bf16[8,32,1024]{2,1,0:T(8,128)(2,1)S(1)}, u32[]{:S(2)}, u32[]{:S(2)}) %collective-permute-start.1) | collective-permute-done | bytes 524320 | tf_op jit(solution)/shard_map/ppermute | solution.py:219
  85.8 1.0 shard_map.122
  87.5 4.8 %collective-permute-done.6 = bf16[128,1024]{1,0:T(8,128)(2,1)} collective-permute-done((bf16[128,1024]{1,0:T(8,128)(2,1)}, bf16[128,1024]{1,0:T(8,128)(2,1)}, u32[]{:S(2)}, u32[]{:S(2)}) %collective-permute-start.6) | collective-permute-done | bytes 262176 | tf_op jit(solution)/shard_map/ppermute | solution.py:219
  92.3 4.1 %all-to-all-start.2 = ((bf16[8,32,1024]{2,1,0:T(8,128)(2,1)}), bf16[8,32,1024]{2,1,0:T(8,128)(2,1)S(1)}, u32[]{:S(2)}, u32[]{:S(2)}) async-start(bf16[8,32,1024]{2,1,0:T(8,128)(2,1)} %shard_map.122), calls=%async_computation.2 | async-start | bytes 1048576 | tf_op jit(solution)/shard_map/all_to_all | solution.py:264
  96.4 1.2 add_convert_fusion.refs_0_
  97.7 1.0 collective-permute-start.8
  98.7 2.2 %collective-permute-start.7 = (bf16[128,1024]{1,0:T(8,128)(2,1)S(1)}, bf16[128,1024]{1,0:T(8,128)(2,1)S(1)}, u32[]{:S(2)}, u32[]{:S(2)}) collective-permute-start(bf16[128,1024]{1,0:T(8,128)(2,1)S(1)} %add_convert_fusion.refs_0_), channel_id=1, source_target_pairs={{0,64},{64,128},{128,192},{192,0},{1,65},{65,129},{129,193},{193,1... | collective-permute-start | bytes 786440 | tf_op jit(solution)/shard_map/ppermute | solution.py:219
  100.9 11.2 %all-to-all-done.2 = bf16[8,32,1024]{2,1,0:T(8,128)(2,1)S(1)} async-done(((bf16[8,32,1024]{2,1,0:T(8,128)(2,1)}), bf16[8,32,1024]{2,1,0:T(8,128)(2,1)S(1)}, u32[]{:S(2)}, u32[]{:S(2)}) %all-to-all-start.2) | async-done | bytes 524320 | tf_op jit(solution)/shard_map/all_to_all | solution.py:264
  112.3 3.2 %collective-permute-start.11 = (bf16[32,1024]{1,0:T(8,128)(2,1)S(1)}, bf16[32,1024]{1,0:T(8,128)(2,1)S(1)}, u32[]{:S(2)}, u32[]{:S(2)}) collective-permute-start(bf16[32,1024]{1,0:T(8,128)(2,1)S(1)} %reduce_sum.12), channel_id=1, source_target_pairs={{0,64},{64,128},{128,192},{192,0},{1,65},{65,129},{129,193},{193,1... | collective-permute-start | bytes 196616 | tf_op jit(solution)/shard_map/ppermute | solution.py:219
  115.6 1.1 shard_map.123
  116.6 1.4 %shard_map.124 = (f32[4,64,1024]{2,1,0:T(8,128)}, f32[4,256,256]{2,1,0:T(8,128)}) custom-call(s32[1]{0:T(128)} %bitcast.3.group_ref, bf16[128,1024]{1,0:T(8,128)(2,1)S(1)} %add_convert_fusion.refs_0_, bf16[128,1024]{1,0:T(8,128)(2,1)S(1)} %collective-permute-done.7.refs_1_, bf16[128,1024]{1,0:T(8,128)(2,1)S(1)} %collective-permute-done.8.refs_2_, ...), custom_call_target="tpu_custom_call" | custom-call | bytes 3000000 | tf_op jit(solution)/shard_map/pallas_call | solution.py:202
  118.1 3.2 %collective-permute-done.10 = bf16[32,1024]{1,0:T(8,128)(2,1)S(1)} collective-permute-done((bf16[32,1024]{1,0:T(8,128)(2,1)S(1)}, bf16[32,1024]{1,0:T(8,128)(2,1)S(1)}, u32[]{:S(2)}, u32[]{:S(2)}) %collective-permute-start.10) | collective-permute-done | bytes 65568 | tf_op jit(solution)/shard_map/ppermute | solution.py:219
  (28 shorter events, 4.6 us)
Async XLA Ops:
  3.0 25.1 %all-to-all-start = ((bf16[64,16,128]{2,1,0:T(8,128)(2,1)}), bf16[64,16,128]{2,1,0:T(8,128)(2,1)S(1)}, u32[]{:S(2)}, u32[]{:S(2)}) async-start(bf16[64,16,128]{2,1,0:T(8,128)(2,1)} %bitcast.13), calls=%async_computation | async-start | bytes 524288 | tf_op jit(solution)/shard_map/all_to_all | solution.py:238
  28.1 0.7 copy-start.4
  48.3 4.5 %collective-permute-start = (bf16[4,8,32,1024]{3,2,1,0:T(8,128)(2,1)}, bf16[4,8,32,1024]{3,2,1,0:T(8,128)(2,1)S(1)}, u32[]{:S(2)}, u32[]{:S(2)}) collective-permute-start(bf16[4,8,32,1024]{3,2,1,0:T(8,128)(2,1)} %get-tuple-element.38), channel_id=1, source_target_pairs={{0,1},{1,0},{2,3},{3,2},{4,5},{5,4},{6,7},{7,6},{8,9},{9,8},{10,11... | collective-permute-start | bytes 6291464 | tf_op jit(solution)/shard_map/ppermute | solution.py:256
  52.7 1.6 %copy-start = (bf16[4,8,32,1024]{3,2,1,0:T(8,128)(2,1)S(1)}, bf16[4,8,32,1024]{3,2,1,0:T(8,128)(2,1)}, u32[]{:S(2)}) copy-start(bf16[4,8,32,1024]{3,2,1,0:T(8,128)(2,1)} %get-tuple-element.37.own_ref) | copy-start | bytes 6291460
  55.7 28.7 %collective-permute-start.1 = (bf16[8,32,1024]{2,1,0:T(8,128)(2,1)}, bf16[8,32,1024]{2,1,0:T(8,128)(2,1)S(1)}, u32[]{:S(2)}, u32[]{:S(2)}) collective-permute-start(bf16[8,32,1024]{2,1,0:T(8,128)(2,1)} %get-tuple-element.49), channel_id=1, source_target_pairs={{0,2},{2,4},{4,6},{6,0},{1,3},{3,5},{5,7},{7,1},{8,10},{10,12},{12... | collective-permute-start | bytes 1572872 | tf_op jit(solution)/shard_map/ppermute | solution.py:219
  56.5 28.7 %collective-permute-start.2 = (bf16[8,32,1024]{2,1,0:T(8,128)(2,1)}, bf16[8,32,1024]{2,1,0:T(8,128)(2,1)S(1)}, u32[]{:S(2)}, u32[]{:S(2)}) collective-permute-start(bf16[8,32,1024]{2,1,0:T(8,128)(2,1)} %get-tuple-element.50), channel_id=1, source_target_pairs={{0,4},{2,6},{4,0},{6,2},{1,5},{3,7},{5,1},{7,3},{8,12},{10,14},{12... | collective-permute-start | bytes 1572872 | tf_op jit(solution)/shard_map/ppermute | solution.py:219
  58.9 26.8 %collective-permute-start.3 = (bf16[8,32,1024]{2,1,0:T(8,128)(2,1)S(1)}, bf16[8,32,1024]{2,1,0:T(8,128)(2,1)S(1)}, u32[]{:S(2)}, u32[]{:S(2)}) collective-permute-start(bf16[8,32,1024]{2,1,0:T(8,128)(2,1)S(1)} %get-tuple-element.51), channel_id=1, source_target_pairs={{0,6},{2,0},{4,2},{6,4},{1,7},{3,1},{5,3},{7,5},{8,14},{10,8},{12,... | collective-permute-start | bytes 1572872 | tf_op jit(solution)/shard_map/ppermute | solution.py:219
  60.4 36.0 %copy-start.2 = (bf16[128,1024]{1,0:T(8,128)(2,1)S(1)}, bf16[128,1024]{1,0:T(8,128)(2,1)}, u32[]{:S(2)}) copy-start(bf16[128,1024]{1,0:T(8,128)(2,1)} %get-tuple-element.58) | copy-start | bytes 786436
  60.4 31.9 %all-to-all-start.1 = ((bf16[64,16,128]{2,1,0:T(8,128)(2,1)}), bf16[64,16,128]{2,1,0:T(8,128)(2,1)S(1)}, u32[]{:S(2)}, u32[]{:S(2)}) async-start(bf16[64,16,128]{2,1,0:T(8,128)(2,1)} %bitcast.11), calls=%async_computation.1 | async-start | bytes 524288 | tf_op jit(solution)/shard_map/all_to_all | solution.py:260
  65.8 21.1 %collective-permute-start.4 = (bf16[128,1024]{1,0:T(8,128)(2,1)}, bf16[128,1024]{1,0:T(8,128)(2,1)S(1)}, u32[]{:S(2)}, u32[]{:S(2)}) collective-permute-start(bf16[128,1024]{1,0:T(8,128)(2,1)} %get-tuple-element.54), channel_id=1, source_target_pairs={{0,64},{64,128},{128,192},{192,0},{1,65},{65,129},{129,193},{193,1... | collective-permute-start | bytes 786440 | tf_op jit(solution)/shard_map/ppermute | solution.py:219
  66.3 20.5 %collective-permute-start.5 = (bf16[128,1024]{1,0:T(8,128)(2,1)}, bf16[128,1024]{1,0:T(8,128)(2,1)S(1)}, u32[]{:S(2)}, u32[]{:S(2)}) collective-permute-start(bf16[128,1024]{1,0:T(8,128)(2,1)} %get-tuple-element.55), channel_id=1, source_target_pairs={{0,128},{64,192},{128,0},{192,64},{1,129},{65,193},{129,1},{193,65... | collective-permute-start | bytes 786440 | tf_op jit(solution)/shard_map/ppermute | solution.py:219
  84.4 7.9 %collective-permute-start.6 = (bf16[128,1024]{1,0:T(8,128)(2,1)}, bf16[128,1024]{1,0:T(8,128)(2,1)}, u32[]{:S(2)}, u32[]{:S(2)}) collective-permute-start(bf16[128,1024]{1,0:T(8,128)(2,1)} %get-tuple-element.56), channel_id=1, source_target_pairs={{0,192},{64,0},{128,64},{192,128},{1,193},{65,1},{129,65},{193,129... | collective-permute-start | bytes 786440 | tf_op jit(solution)/shard_map/ppermute | solution.py:219
  86.8 28.7 %copy-start.1 = (s32[1,384]{1,0:T(1,128)S(1)}, s32[1,384]{1,0:T(1,128)}, u32[]{:S(2)}) copy-start(s32[1,384]{1,0:T(1,128)} %get-tuple-element.35.target_ref) | copy-start | bytes 4612
  86.8 0.7 copy-start.3
  92.3 19.8 %all-to-all-start.2 = ((bf16[8,32,1024]{2,1,0:T(8,128)(2,1)}), bf16[8,32,1024]{2,1,0:T(8,128)(2,1)S(1)}, u32[]{:S(2)}, u32[]{:S(2)}) async-start(bf16[8,32,1024]{2,1,0:T(8,128)(2,1)} %shard_map.122), calls=%async_computation.2 | async-start | bytes 1048576 | tf_op jit(solution)/shard_map/all_to_all | solution.py:264
  97.6 18.0 %collective-permute-start.9 = (bf16[128,1024]{1,0:T(8,128)(2,1)S(1)}, bf16[128,1024]{1,0:T(8,128)(2,1)S(1)}, u32[]{:S(2)}, u32[]{:S(2)}) collective-permute-start(bf16[128,1024]{1,0:T(8,128)(2,1)S(1)} %add_convert_fusion.refs_0_), channel_id=1, source_target_pairs={{0,192},{64,0},{128,64},{192,128},{1,193},{65,1},{129,65},{193,129... | collective-permute-start | bytes 786440 | tf_op jit(solution)/shard_map/ppermute | solution.py:219
  97.7 18.9 %collective-permute-start.8 = (bf16[128,1024]{1,0:T(8,128)(2,1)S(1)}, bf16[128,1024]{1,0:T(8,128)(2,1)S(1)}, u32[]{:S(2)}, u32[]{:S(2)}) collective-permute-start(bf16[128,1024]{1,0:T(8,128)(2,1)S(1)} %add_convert_fusion.refs_0_), channel_id=1, source_target_pairs={{0,128},{64,192},{128,0},{192,64},{1,129},{65,193},{129,1},{193,65... | collective-permute-start | bytes 786440 | tf_op jit(solution)/shard_map/ppermute | solution.py:219
  98.7 18.0 %collective-permute-start.7 = (bf16[128,1024]{1,0:T(8,128)(2,1)S(1)}, bf16[128,1024]{1,0:T(8,128)(2,1)S(1)}, u32[]{:S(2)}, u32[]{:S(2)}) collective-permute-start(bf16[128,1024]{1,0:T(8,128)(2,1)S(1)} %add_convert_fusion.refs_0_), channel_id=1, source_target_pairs={{0,64},{64,128},{128,192},{192,0},{1,65},{65,129},{129,193},{193,1... | collective-permute-start | bytes 786440 | tf_op jit(solution)/shard_map/ppermute | solution.py:219
  112.2 5.8 %collective-permute-start.12 = (bf16[32,1024]{1,0:T(8,128)(2,1)S(1)}, bf16[32,1024]{1,0:T(8,128)(2,1)S(1)}, u32[]{:S(2)}, u32[]{:S(2)}) collective-permute-start(bf16[32,1024]{1,0:T(8,128)(2,1)S(1)} %reduce_sum.12), channel_id=1, source_target_pairs={{0,192},{64,0},{128,64},{192,128},{1,193},{65,1},{129,65},{193,129... | collective-permute-start | bytes 196616 | tf_op jit(solution)/shard_map/ppermute | solution.py:219
  112.3 5.8 %collective-permute-start.11 = (bf16[32,1024]{1,0:T(8,128)(2,1)S(1)}, bf16[32,1024]{1,0:T(8,128)(2,1)S(1)}, u32[]{:S(2)}, u32[]{:S(2)}) collective-permute-start(bf16[32,1024]{1,0:T(8,128)(2,1)S(1)} %reduce_sum.12), channel_id=1, source_target_pairs={{0,64},{64,128},{128,192},{192,0},{1,65},{65,129},{129,193},{193,1... | collective-permute-start | bytes 196616 | tf_op jit(solution)/shard_map/ppermute | solution.py:219
  115.6 5.8 %collective-permute-start.10 = (bf16[32,1024]{1,0:T(8,128)(2,1)S(1)}, bf16[32,1024]{1,0:T(8,128)(2,1)S(1)}, u32[]{:S(2)}, u32[]{:S(2)}) collective-permute-start(bf16[32,1024]{1,0:T(8,128)(2,1)S(1)} %reduce_sum.12), channel_id=1, source_target_pairs={{0,128},{64,192},{128,0},{192,64},{1,129},{65,193},{129,1},{193,65... | collective-permute-start | bytes 196616 | tf_op jit(solution)/shard_map/ppermute | solution.py:219

commit v4 on v3

--- a/solution.py
+++ b/solution.py
@@ -182,15 +182,26 @@
             out_ref[at, 64 * q : 64 * q + 64] = shares[k][64:, TILE * q : TILE * q + TILE].astype(F32)
 
 
-def pair_sum_kernel(y_ref, own_ref, got_ref, *out_refs):
-    for k, out_ref in enumerate(out_refs):
+def pair_sum_kernel(y_ref, own_ref, got_ref, mine_ref, *out_refs):
+    for k in range(YS):
         at = lax.rem(y_ref[0] + k, YS)
-        out_ref[...] = (own_ref[at].astype(F32) + got_ref[at].astype(F32)).astype(BF)
-
-
-def plane_sum_kernel(a_ref, b_ref, c_ref, d_ref, out_ref):
-    a, b, c, d = [r[...].astype(F32) for r in (a_ref, b_ref, c_ref, d_ref)]
-    out_ref[...] = ((a + b) + (c + d)).astype(BF)
+        total = (own_ref[at].astype(F32) + got_ref[at].astype(F32)).astype(BF)
+        if k == 0:
+            mine_ref[...] = total
+        else:
+            out_refs[2 * k - 2][...] = total[:, :16]
+            out_refs[2 * k - 1][...] = total[:, 16:]
+
+
+def relay_kernel(up_ref, got_up_ref, down_ref, got_down_ref, up_out_ref, down_out_ref):
+    up_out_ref[...] = (up_ref[...].astype(F32) + got_up_ref[...].astype(F32)).astype(BF)
+    down_out_ref[...] = (down_ref[...].astype(F32) + got_down_ref[...].astype(F32)).astype(BF)
+
+
+def plane_sum_kernel(mine_ref, up1_ref, down1_ref, up2_ref, down2_ref, out_ref):
+    for at, up_ref, down_ref in ((0, up1_ref, down1_ref), (16, up2_ref, down2_ref)):
+        mine = mine_ref[:, at : at + 16].astype(F32)
+        out_ref[:, at : at + 16] = (mine + (up_ref[...].astype(F32) + down_ref[...].astype(F32))).astype(BF)
 
 
 VM = pl.BlockSpec(memory_space=pltpu.VMEM)
@@ -252,14 +263,23 @@
     )
     block_parts, (send, own) = rest[:4], rest[4:]
     y_at = lax.axis_index("y").astype(jnp.int32).reshape(1)
+    chunk = ((ZS, 16, lat), BF)
     parts = call(
-        pair_sum_kernel, [((ZS, 32, lat), BF)] * YS, y_at, own, lax.ppermute(send, "core", ring(CS, 1)),
+        pair_sum_kernel, [((ZS, 32, lat), BF)] + [chunk] * 6, y_at, own, lax.ppermute(send, "core", ring(CS, 1)),
         smem=1, vmem=10, moved=8_000_000,
     )
     parts, block_parts, back = lax.optimization_barrier((parts, block_parts, back))
     returned = lax.all_to_all(back, session, split_axis=0, concat_axis=0, tiled=True)
     block_terms = others(block_parts, "group")
-    (mine,) = call(plane_sum_kernel, [((ZS, 32, lat), BF)], *others(parts, "y"), vmem=6, moved=3_000_000)
+    mine, next1, next2, two1, two2, last1, last2 = parts
+    up, down = ring(YS, 1), ring(YS, YS - 1)
+    got_up, got_down = lax.ppermute(two1, "y", up), lax.ppermute(two2, "y", down)
+    up2, down1 = lax.ppermute(next2, "y", up), lax.ppermute(last1, "y", down)
+    relay_up, relay_down = call(relay_kernel, [chunk] * 2, next1, got_up, last2, got_down, vmem=6, moved=2_000_000)
+    up1, down2 = lax.ppermute(relay_up, "y", up), lax.ppermute(relay_down, "y", down)
+    (mine,) = call(
+        plane_sum_kernel, [((ZS, 32, lat), BF)], mine, up1, down1, up2, down2, vmem=6, moved=3_000_000
+    )
     mine, returned, block_terms = lax.optimization_barrier((mine, returned, block_terms))
     layer_terms = lax.all_to_all(mine, "z", split_axis=0, concat_axis=0, tiled=True)
     share = add_all(block_terms).astype(BF)

time: 122 us -> 119 us (0.975)
  waiting for transfers between devices: 52.6 us -> 45.5 us
  starting transfers between devices: 37 us -> 41.9 us
    ppermute x12 -> x9, waiting for transfers between devices: 24.2 us -> 8.19 us  [others(): lax.ppermute(parts[k], axis, ring(n, k))]
    ppermute x0 -> x6, starting transfers between devices: none -> 8.58 us  [the longest x1 2.4 us: on_device(): lax.ppermute(two2, 'y', down)]
    ppermute x0 -> x6, waiting for transfers between devices: none -> 8.25 us  [the longest x1 4.68 us: on_device(): lax.ppermute(relay_up, 'y', up)]
    ppermute x12 -> x9, starting transfers between devices: 15.1 us -> 9.73 us  [others(): lax.ppermute(parts[k], axis, ring(n, k))]
    all_to_all x1, starting transfers between devices: 4.08 us -> 6.16 us  [on_device(): lax.all_to_all(mine, 'z', split_axis=0, concat_axis=0, tiled=True)]
    unnamed x10 -> x6, local copies, waits for them, and re-layouts: 3 us -> 2.3 us
    pallas_call x6 -> x7, Pallas kernels: 26.8 us -> 26.7 us  [call(): pl.pallas_call(kernel, out_shape=[jax.ShapeDtypeStruct(s, d) for s, d in...]
  transfers between devices with their start and end apart: 16 -> 19, of which waited for: 7 -> 9; matrix products, arithmetic and copies ran while one was open for 1% -> 1% of each run, Pallas kernels for 3% -> 3%
where the time goes in v4:
time: 119 us
  waiting for transfers between devices  45.5 us (38%)
  starting transfers between devices  41.9 us (35%)
  Pallas kernels  26.7 us (22%)
  local copies, waits for them, and re-layouts  2.96 us (2%)
  other arithmetic  1.31 us (1%)
    pallas_call x7, Pallas kernels, call(): pl.pallas_call(kernel, out_shape=[jax.ShapeDtypeStruct(s, d) for s, d in...  26.7 us
    all_to_all x1, waiting for transfers between devices, on_device(): lax.all_to_all(packed, session, split_axis=0, concat_axis=0, tiled=True)  13 us
    all_to_all x1, starting transfers between devices, on_device(): lax.all_to_all(packed, session, split_axis=0, concat_axis=0, tiled=True)  12.1 us
    all_to_all x1, waiting for transfers between devices, on_device(): lax.all_to_all(mine, 'z', split_axis=0, concat_axis=0, tiled=True)  12 us
    ppermute x9, starting transfers between devices, others(): lax.ppermute(parts[k], axis, ring(n, k))  9.73 us
    ppermute x9, waiting for transfers between devices, others(): lax.ppermute(parts[k], axis, ring(n, k))  8.19 us
    all_to_all x1, starting transfers between devices, on_device(): lax.all_to_all(mine, 'z', split_axis=0, concat_axis=0, tiled=True)  6.16 us
    all_to_all x1, starting transfers between devices, on_device(): lax.all_to_all(back, session, split_axis=0, concat_axis=0, tiled=True)  4.99 us
  transfers between devices with their start and end apart: 19, of which 9 were waited for; matrix products, arithmetic and copies ran while one was open for 1% of the time, Pallas kernels for 3%

profile of v4, /device:TPU:6, one launch (start us, length us, event | category | flops | bytes accessed | tf_op | source)
XLA Modules:
  0.0 119.1 jit_solution(14449135564741155817)
XLA Ops:
  0.6 2.4 %shard_map.119 = (bf16[1024,128]{1,0:T(8,128)(2,1)}, s32[1,384]{1,0:T(1,128)}) custom-call(s32[1,384]{1,0:T(1,128)} %bitcast.14, s32[384]{0:T(512)} %block_ref.1, bf16[384,128]{1,0:T(8,128)(2,1)} %spikes_ref.1), custom_call_target="tpu_custom_call" | custom-call | tf_op jit(solution)/shard_map/pallas_call | solution.py:213
  3.0 12.1 %all-to-all-start = ((bf16[64,16,128]{2,1,0:T(8,128)(2,1)}), bf16[64,16,128]{2,1,0:T(8,128)(2,1)S(1)}, u32[]{:S(2)}, u32[]{:S(2)}) async-start(bf16[64,16,128]{2,1,0:T(8,128)(2,1)} %bitcast.13), calls=%async_computation | async-start | bytes 524288 | tf_op jit(solution)/shard_map/all_to_all | solution.py:249
  15.1 13.0 %all-to-all-done = bf16[64,16,128]{2,1,0:T(8,128)(2,1)S(1)} async-done(((bf16[64,16,128]{2,1,0:T(8,128)(2,1)}), bf16[64,16,128]{2,1,0:T(8,128)(2,1)S(1)}, u32[]{:S(2)}, u32[]{:S(2)}) %all-to-all-start) | async-done | bytes 262176 | tf_op jit(solution)/shard_map/all_to_all | solution.py:249
  28.8 19.5 %shard_map.120 = (bf16[1024,128]{1,0:T(8,128)(2,1)}, bf16[128,1024]{1,0:T(8,128)(2,1)}, bf16[128,1024]{1,0:T(8,128)(2,1)}, bf16[128,1024]{1,0:T(8,128)(2,1)}, bf...) custom-call(s32[1]{0:T(128)} %bitcast.2.core_ref, s32[1]{0:T(128)} %bitcast.3.group_ref, ...), custom_call_target="tpu_custom_call" | custom-call | flops 12000000000 | bytes 12000000 | tf_op jit(solution)/shard_map/pallas_call | solution.py:213
  48.6 4.1 %collective-permute-done.got_ref = bf16[4,8,32,1024]{3,2,1,0:T(8,128)(2,1)S(1)} collective-permute-done((bf16[4,8,32,1024]{3,2,1,0:T(8,128)(2,1)}, bf16[4,8,32,1024]{3,2,1,0:T(8,128)(2,1)S(1)}, u32[]{:S(2)}, u32[]{:S(2)}) %collective-permute-start) | collective-permute-done | bytes 2097184 | tf_op jit(solution)/shard_map/ppermute | solution.py:268
  52.8 1.6 %copy-done = bf16[4,8,32,1024]{3,2,1,0:T(8,128)(2,1)S(1)} copy-done((bf16[4,8,32,1024]{3,2,1,0:T(8,128)(2,1)S(1)}, bf16[4,8,32,1024]{3,2,1,0:T(8,128)(2,1)}, u32[]{:S(2)}) %copy-start) | copy-done | bytes 2097176
  54.3 1.2 %shard_map.121 = (bf16[8,32,1024]{2,1,0:T(8,128)(2,1)S(1)}, bf16[8,16,1024]{2,1,0:T(8,128)(2,1)S(1)}, bf16[8,16,1024]{2,1,0:T(8,128)(2,1)S(1)}, bf16[8,16,1024]{...) custom-call(s32[1]{0:T(128)} %bitcast.1.y_ref, ...), custom_call_target="tpu_custom_call" | custom-call | bytes 8000000 | tf_op jit(solution)/shard_map/pallas_call | solution.py:213
  56.4 2.4 %collective-permute-start.2 = (bf16[8,16,1024]{2,1,0:T(8,128)(2,1)}, bf16[8,16,1024]{2,1,0:T(8,128)(2,1)S(1)}, u32[]{:S(2)}, u32[]{:S(2)}) collective-permute-start(bf16[8,16,1024]{2,1,0:T(8,128)(2,1)} %get-tuple-element.63), channel_id=1, source_target_pairs={{0,6},{2,0},{4,2},{6,4},{1,7},{3,1},{5,3},{7,5},{8,14},{10,8},{12,... | collective-permute-start | bytes 786440 | tf_op jit(solution)/shard_map/ppermute | solution.py:276
  59.3 1.5 %collective-permute-start.5 = (bf16[8,16,1024]{2,1,0:T(8,128)(2,1)S(1)}, bf16[8,16,1024]{2,1,0:T(8,128)(2,1)S(1)}, u32[]{:S(2)}, u32[]{:S(2)}) collective-permute-start(bf16[8,16,1024]{2,1,0:T(8,128)(2,1)S(1)} %get-tuple-element.66), channel_id=1, source_target_pairs={{0,2},{2,4},{4,6},{6,0},{1,3},{3,5},{5,7},{7,1},{8,10},{10,12},{12... | collective-permute-start | bytes 786440 | tf_op jit(solution)/shard_map/ppermute | solution.py:277
  60.8 5.0 %all-to-all-start.1 = ((bf16[64,16,128]{2,1,0:T(8,128)(2,1)}), bf16[64,16,128]{2,1,0:T(8,128)(2,1)S(1)}, u32[]{:S(2)}, u32[]{:S(2)}) async-start(bf16[64,16,128]{2,1,0:T(8,128)(2,1)} %bitcast.11), calls=%async_computation.1 | async-start | bytes 524288 | tf_op jit(solution)/shard_map/all_to_all | solution.py:272
  66.5 1.6 %collective-permute-start.3 = (bf16[8,16,1024]{2,1,0:T(8,128)(2,1)S(1)}, bf16[8,16,1024]{2,1,0:T(8,128)(2,1)S(1)}, u32[]{:S(2)}, u32[]{:S(2)}) collective-permute-start(bf16[8,16,1024]{2,1,0:T(8,128)(2,1)S(1)} %get-tuple-element.64), channel_id=1, source_target_pairs={{0,2},{2,4},{4,6},{6,0},{1,3},{3,5},{5,7},{7,1},{8,10},{10,12},{12... | collective-permute-start | bytes 786440 | tf_op jit(solution)/shard_map/ppermute | solution.py:279
  68.2 1.7 %collective-permute-start.6 = (bf16[8,16,1024]{2,1,0:T(8,128)(2,1)S(1)}, bf16[8,16,1024]{2,1,0:T(8,128)(2,1)S(1)}, u32[]{:S(2)}, u32[]{:S(2)}) collective-permute-start(bf16[8,16,1024]{2,1,0:T(8,128)(2,1)S(1)} %get-tuple-element.67), channel_id=1, source_target_pairs={{0,6},{2,0},{4,2},{6,4},{1,7},{3,1},{5,3},{7,5},{8,14},{10,8},{12,... | collective-permute-start | bytes 786440 | tf_op jit(solution)/shard_map/ppermute | solution.py:279
  69.8 3.6 %collective-permute-done.4.down1_ref = bf16[8,16,1024]{2,1,0:T(8,128)(2,1)S(1)} collective-permute-done((bf16[8,16,1024]{2,1,0:T(8,128)(2,1)}, bf16[8,16,1024]{2,1,0:T(8,128)(2,1)S(1)}, u32[]{:S(2)}, u32[]{:S(2)}) %collective-permute-start.4) | collective-permute-done | bytes 262176 | tf_op jit(solution)/shard_map/ppermute | solution.py:277
  73.4 1.4 %collective-permute-start.8 = (bf16[128,1024]{1,0:T(8,128)(2,1)}, bf16[128,1024]{1,0:T(8,128)(2,1)S(1)}, u32[]{:S(2)}, u32[]{:S(2)}) collective-permute-start(bf16[128,1024]{1,0:T(8,128)(2,1)} %get-tuple-element.71), channel_id=1, source_target_pairs={{0,128},{64,192},{128,0},{192,64},{1,129},{65,193},{129,1},{193,65... | collective-permute-start | bytes 786440 | tf_op jit(solution)/shard_map/ppermute | solution.py:230
  74.8 4.7 %collective-permute-done.3.up1_ref = bf16[8,16,1024]{2,1,0:T(8,128)(2,1)S(1)} collective-permute-done((bf16[8,16,1024]{2,1,0:T(8,128)(2,1)S(1)}, bf16[8,16,1024]{2,1,0:T(8,128)(2,1)S(1)}, u32[]{:S(2)}, u32[]{:S(2)}) %collective-permute-start.3) | collective-permute-done | bytes 262176 | tf_op jit(solution)/shard_map/ppermute | solution.py:279
  80.5 2.3 %collective-permute-done.8 = bf16[128,1024]{1,0:T(8,128)(2,1)S(1)} collective-permute-done((bf16[128,1024]{1,0:T(8,128)(2,1)}, bf16[128,1024]{1,0:T(8,128)(2,1)S(1)}, u32[]{:S(2)}, u32[]{:S(2)}) %collective-permute-start.8) | collective-permute-done | bytes 262176 | tf_op jit(solution)/shard_map/ppermute | solution.py:230
  82.7 2.7 %collective-permute-done.9 = bf16[128,1024]{1,0:T(8,128)(2,1)S(1)} collective-permute-done((bf16[128,1024]{1,0:T(8,128)(2,1)}, bf16[128,1024]{1,0:T(8,128)(2,1)S(1)}, u32[]{:S(2)}, u32[]{:S(2)}) %collective-permute-start.9) | collective-permute-done | bytes 262176 | tf_op jit(solution)/shard_map/ppermute | solution.py:230
  85.4 6.2 %all-to-all-start.2 = ((bf16[8,32,1024]{2,1,0:T(8,128)(2,1)}), bf16[8,32,1024]{2,1,0:T(8,128)(2,1)S(1)}, u32[]{:S(2)}, u32[]{:S(2)}) async-start(bf16[8,32,1024]{2,1,0:T(8,128)(2,1)} %shard_map.123), calls=%async_computation.2 | async-start | bytes 1048576 | tf_op jit(solution)/shard_map/all_to_all | solution.py:284
  91.5 1.2 %add_convert_fusion.refs_0_ = bf16[128,1024]{1,0:T(8,128)(2,1)S(1)} fusion(bf16[128,1024]{1,0:T(8,128)(2,1)S(1)} %collective-permute-done.9, bf16[128,1024]{1,0:T(8,128)(2,1)} %collective-permute-done.7, bf16[128,1024]{1,0:T(8,128)(2,1)S(1)} %collective-permute-done.8, bf16[128,1024]{1,0:T(8,128)(2,1)} %get-tuple-element.74), kind=kLoop, calls=%fused_computation | loop fusion | flops 1048576 | bytes 1310720 | tf_op jit(solution)/shard_map/convert_element_type | solution.py:285
  94.9 2.3 %collective-permute-start.10 = (bf16[128,1024]{1,0:T(8,128)(2,1)S(1)}, bf16[128,1024]{1,0:T(8,128)(2,1)S(1)}, u32[]{:S(2)}, u32[]{:S(2)}) collective-permute-start(bf16[128,1024]{1,0:T(8,128)(2,1)S(1)} %add_convert_fusion.refs_0_), channel_id=1, source_target_pairs={{0,64},{64,128},{128,192},{192,0},{1,65},{65,129},{129,193},{193,1... | collective-permute-start | bytes 786440 | tf_op jit(solution)/shard_map/ppermute | solution.py:230
  97.2 12.0 %all-to-all-done.2 = bf16[8,32,1024]{2,1,0:T(8,128)(2,1)S(1)} async-done(((bf16[8,32,1024]{2,1,0:T(8,128)(2,1)}), bf16[8,32,1024]{2,1,0:T(8,128)(2,1)S(1)}, u32[]{:S(2)}, u32[]{:S(2)}) %all-to-all-start.2) | async-done | bytes 524320 | tf_op jit(solution)/shard_map/all_to_all | solution.py:284
  109.4 3.2 %collective-permute-start.14 = (bf16[32,1024]{1,0:T(8,128)(2,1)S(1)}, bf16[32,1024]{1,0:T(8,128)(2,1)S(1)}, u32[]{:S(2)}, u32[]{:S(2)}) collective-permute-start(bf16[32,1024]{1,0:T(8,128)(2,1)S(1)} %reduce_sum.12), channel_id=1, source_target_pairs={{0,64},{64,128},{128,192},{192,0},{1,65},{65,129},{129,193},{193,1... | collective-permute-start | bytes 196616 | tf_op jit(solution)/shard_map/ppermute | solution.py:230
  113.7 1.4 %shard_map.125 = (f32[4,64,1024]{2,1,0:T(8,128)}, f32[4,256,256]{2,1,0:T(8,128)}) custom-call(s32[1]{0:T(128)} %bitcast.3.group_ref, bf16[128,1024]{1,0:T(8,128)(2,1)S(1)} %add_convert_fusion.refs_0_, bf16[128,1024]{1,0:T(8,128)(2,1)S(1)} %collective-permute-done.10.refs_1_, bf16[128,1024]{1,0:T(8,128)(2,1)S(1)} %collective-permute-done.11.refs_2_, ...), custom_call_target="tpu_custom_call" | custom-call | bytes 3000000 | tf_op jit(solution)/shard_map/pallas_call | solution.py:213
  115.3 3.1 %collective-permute-done.13 = bf16[32,1024]{1,0:T(8,128)(2,1)S(1)} collective-permute-done((bf16[32,1024]{1,0:T(8,128)(2,1)S(1)}, bf16[32,1024]{1,0:T(8,128)(2,1)S(1)}, u32[]{:S(2)}, u32[]{:S(2)}) %collective-permute-start.13) | collective-permute-done | bytes 65568 | tf_op jit(solution)/shard_map/ppermute | solution.py:230
  (31 shorter events, 8.4 us)
Async XLA Ops:
  3.0 25.1 %all-to-all-start = ((bf16[64,16,128]{2,1,0:T(8,128)(2,1)}), bf16[64,16,128]{2,1,0:T(8,128)(2,1)S(1)}, u32[]{:S(2)}, u32[]{:S(2)}) async-start(bf16[64,16,128]{2,1,0:T(8,128)(2,1)} %bitcast.13), calls=%async_computation | async-start | bytes 524288 | tf_op jit(solution)/shard_map/all_to_all | solution.py:249
  28.1 0.7 copy-start.2
  48.3 4.5 %collective-permute-start = (bf16[4,8,32,1024]{3,2,1,0:T(8,128)(2,1)}, bf16[4,8,32,1024]{3,2,1,0:T(8,128)(2,1)S(1)}, u32[]{:S(2)}, u32[]{:S(2)}) collective-permute-start(bf16[4,8,32,1024]{3,2,1,0:T(8,128)(2,1)} %get-tuple-element.46), channel_id=1, source_target_pairs={{0,1},{1,0},{2,3},{3,2},{4,5},{5,4},{6,7},{7,6},{8,9},{9,8},{10,11... | collective-permute-start | bytes 6291464 | tf_op jit(solution)/shard_map/ppermute | solution.py:268
  52.8 1.6 %copy-start = (bf16[4,8,32,1024]{3,2,1,0:T(8,128)(2,1)S(1)}, bf16[4,8,32,1024]{3,2,1,0:T(8,128)(2,1)}, u32[]{:S(2)}) copy-start(bf16[4,8,32,1024]{3,2,1,0:T(8,128)(2,1)} %get-tuple-element.45.own_ref) | copy-start | bytes 6291460
  55.5 10.8 %collective-permute-start.1 = (bf16[8,16,1024]{2,1,0:T(8,128)(2,1)}, bf16[8,16,1024]{2,1,0:T(8,128)(2,1)S(1)}, u32[]{:S(2)}, u32[]{:S(2)}) collective-permute-start(bf16[8,16,1024]{2,1,0:T(8,128)(2,1)} %get-tuple-element.61), channel_id=1, source_target_pairs={{0,2},{2,4},{4,6},{6,0},{1,3},{3,5},{5,7},{7,1},{8,10},{10,12},{12... | collective-permute-start | bytes 786440 | tf_op jit(solution)/shard_map/ppermute | solution.py:276
  56.4 10.0 %collective-permute-start.2 = (bf16[8,16,1024]{2,1,0:T(8,128)(2,1)}, bf16[8,16,1024]{2,1,0:T(8,128)(2,1)S(1)}, u32[]{:S(2)}, u32[]{:S(2)}) collective-permute-start(bf16[8,16,1024]{2,1,0:T(8,128)(2,1)} %get-tuple-element.63), channel_id=1, source_target_pairs={{0,6},{2,0},{4,2},{6,4},{1,7},{3,1},{5,3},{7,5},{8,14},{10,8},{12,... | collective-permute-start | bytes 786440 | tf_op jit(solution)/shard_map/ppermute | solution.py:276
  58.8 14.6 %collective-permute-start.4 = (bf16[8,16,1024]{2,1,0:T(8,128)(2,1)}, bf16[8,16,1024]{2,1,0:T(8,128)(2,1)S(1)}, u32[]{:S(2)}, u32[]{:S(2)}) collective-permute-start(bf16[8,16,1024]{2,1,0:T(8,128)(2,1)} %get-tuple-element.65), channel_id=1, source_target_pairs={{0,6},{2,0},{4,2},{6,4},{1,7},{3,1},{5,3},{7,5},{8,14},{10,8},{12,... | collective-permute-start | bytes 786440 | tf_op jit(solution)/shard_map/ppermute | solution.py:277
  59.3 15.4 %collective-permute-start.5 = (bf16[8,16,1024]{2,1,0:T(8,128)(2,1)S(1)}, bf16[8,16,1024]{2,1,0:T(8,128)(2,1)S(1)}, u32[]{:S(2)}, u32[]{:S(2)}) collective-permute-start(bf16[8,16,1024]{2,1,0:T(8,128)(2,1)S(1)} %get-tuple-element.66), channel_id=1, source_target_pairs={{0,2},{2,4},{4,6},{6,0},{1,3},{3,5},{5,7},{7,1},{8,10},{10,12},{12... | collective-permute-start | bytes 786440 | tf_op jit(solution)/shard_map/ppermute | solution.py:277
  60.8 24.6 %all-to-all-start.1 = ((bf16[64,16,128]{2,1,0:T(8,128)(2,1)}), bf16[64,16,128]{2,1,0:T(8,128)(2,1)S(1)}, u32[]{:S(2)}, u32[]{:S(2)}) async-start(bf16[64,16,128]{2,1,0:T(8,128)(2,1)} %bitcast.11), calls=%async_computation.1 | async-start | bytes 524288 | tf_op jit(solution)/shard_map/all_to_all | solution.py:272
  65.8 14.6 %collective-permute-start.7 = (bf16[128,1024]{1,0:T(8,128)(2,1)}, bf16[128,1024]{1,0:T(8,128)(2,1)}, u32[]{:S(2)}, u32[]{:S(2)}) collective-permute-start(bf16[128,1024]{1,0:T(8,128)(2,1)} %get-tuple-element.70), channel_id=1, source_target_pairs={{0,64},{64,128},{128,192},{192,0},{1,65},{65,129},{129,193},{193,1... | collective-permute-start | bytes 786440 | tf_op jit(solution)/shard_map/ppermute | solution.py:230
  66.5 13.0 %collective-permute-start.3 = (bf16[8,16,1024]{2,1,0:T(8,128)(2,1)S(1)}, bf16[8,16,1024]{2,1,0:T(8,128)(2,1)S(1)}, u32[]{:S(2)}, u32[]{:S(2)}) collective-permute-start(bf16[8,16,1024]{2,1,0:T(8,128)(2,1)S(1)} %get-tuple-element.64), channel_id=1, source_target_pairs={{0,2},{2,4},{4,6},{6,0},{1,3},{3,5},{5,7},{7,1},{8,10},{10,12},{12... | collective-permute-start | bytes 786440 | tf_op jit(solution)/shard_map/ppermute | solution.py:279
  68.2 44.5 %copy-start.1 = (s32[1,384]{1,0:T(1,128)S(1)}, s32[1,384]{1,0:T(1,128)}, u32[]{:S(2)}) copy-start(s32[1,384]{1,0:T(1,128)} %get-tuple-element.43.target_ref) | copy-start | bytes 4612
  68.2 11.3 %collective-permute-start.6 = (bf16[8,16,1024]{2,1,0:T(8,128)(2,1)S(1)}, bf16[8,16,1024]{2,1,0:T(8,128)(2,1)S(1)}, u32[]{:S(2)}, u32[]{:S(2)}) collective-permute-start(bf16[8,16,1024]{2,1,0:T(8,128)(2,1)S(1)} %get-tuple-element.67), channel_id=1, source_target_pairs={{0,6},{2,0},{4,2},{6,4},{1,7},{3,1},{5,3},{7,5},{8,14},{10,8},{12,... | collective-permute-start | bytes 786440 | tf_op jit(solution)/shard_map/ppermute | solution.py:279
  73.4 9.3 %collective-permute-start.8 = (bf16[128,1024]{1,0:T(8,128)(2,1)}, bf16[128,1024]{1,0:T(8,128)(2,1)S(1)}, u32[]{:S(2)}, u32[]{:S(2)}) collective-permute-start(bf16[128,1024]{1,0:T(8,128)(2,1)} %get-tuple-element.71), channel_id=1, source_target_pairs={{0,128},{64,192},{128,0},{192,64},{1,129},{65,193},{129,1},{193,65... | collective-permute-start | bytes 786440 | tf_op jit(solution)/shard_map/ppermute | solution.py:230
  74.8 10.6 %collective-permute-start.9 = (bf16[128,1024]{1,0:T(8,128)(2,1)}, bf16[128,1024]{1,0:T(8,128)(2,1)S(1)}, u32[]{:S(2)}, u32[]{:S(2)}) collective-permute-start(bf16[128,1024]{1,0:T(8,128)(2,1)} %get-tuple-element.72), channel_id=1, source_target_pairs={{0,192},{64,0},{128,64},{192,128},{1,193},{65,1},{129,65},{193,129... | collective-permute-start | bytes 786440 | tf_op jit(solution)/shard_map/ppermute | solution.py:230
  85.4 23.8 %all-to-all-start.2 = ((bf16[8,32,1024]{2,1,0:T(8,128)(2,1)}), bf16[8,32,1024]{2,1,0:T(8,128)(2,1)S(1)}, u32[]{:S(2)}, u32[]{:S(2)}) async-start(bf16[8,32,1024]{2,1,0:T(8,128)(2,1)} %shard_map.123), calls=%async_computation.2 | async-start | bytes 1048576 | tf_op jit(solution)/shard_map/all_to_all | solution.py:284
  92.7 19.9 %collective-permute-start.12 = (bf16[128,1024]{1,0:T(8,128)(2,1)S(1)}, bf16[128,1024]{1,0:T(8,128)(2,1)S(1)}, u32[]{:S(2)}, u32[]{:S(2)}) collective-permute-start(bf16[128,1024]{1,0:T(8,128)(2,1)S(1)} %add_convert_fusion.refs_0_), channel_id=1, source_target_pairs={{0,192},{64,0},{128,64},{192,128},{1,193},{65,1},{129,65},{193,129... | collective-permute-start | bytes 786440 | tf_op jit(solution)/shard_map/ppermute | solution.py:230
  93.8 19.9 %collective-permute-start.11 = (bf16[128,1024]{1,0:T(8,128)(2,1)S(1)}, bf16[128,1024]{1,0:T(8,128)(2,1)S(1)}, u32[]{:S(2)}, u32[]{:S(2)}) collective-permute-start(bf16[128,1024]{1,0:T(8,128)(2,1)S(1)} %add_convert_fusion.refs_0_), channel_id=1, source_target_pairs={{0,128},{64,192},{128,0},{192,64},{1,129},{65,193},{129,1},{193,65... | collective-permute-start | bytes 786440 | tf_op jit(solution)/shard_map/ppermute | solution.py:230
  94.9 18.8 %collective-permute-start.10 = (bf16[128,1024]{1,0:T(8,128)(2,1)S(1)}, bf16[128,1024]{1,0:T(8,128)(2,1)S(1)}, u32[]{:S(2)}, u32[]{:S(2)}) collective-permute-start(bf16[128,1024]{1,0:T(8,128)(2,1)S(1)} %add_convert_fusion.refs_0_), channel_id=1, source_target_pairs={{0,64},{64,128},{128,192},{192,0},{1,65},{65,129},{129,193},{193,1... | collective-permute-start | bytes 786440 | tf_op jit(solution)/shard_map/ppermute | solution.py:230
  109.3 5.8 %collective-permute-start.15 = (bf16[32,1024]{1,0:T(8,128)(2,1)S(1)}, bf16[32,1024]{1,0:T(8,128)(2,1)S(1)}, u32[]{:S(2)}, u32[]{:S(2)}) collective-permute-start(bf16[32,1024]{1,0:T(8,128)(2,1)S(1)} %reduce_sum.12), channel_id=1, source_target_pairs={{0,192},{64,0},{128,64},{192,128},{1,193},{65,1},{129,65},{193,129... | collective-permute-start | bytes 196616 | tf_op jit(solution)/shard_map/ppermute | solution.py:230
  109.4 5.9 %collective-permute-start.14 = (bf16[32,1024]{1,0:T(8,128)(2,1)S(1)}, bf16[32,1024]{1,0:T(8,128)(2,1)S(1)}, u32[]{:S(2)}, u32[]{:S(2)}) collective-permute-start(bf16[32,1024]{1,0:T(8,128)(2,1)S(1)} %reduce_sum.12), channel_id=1, source_target_pairs={{0,64},{64,128},{128,192},{192,0},{1,65},{65,129},{129,193},{193,1... | collective-permute-start | bytes 196616 | tf_op jit(solution)/shard_map/ppermute | solution.py:230
  112.6 5.8 %collective-permute-start.13 = (bf16[32,1024]{1,0:T(8,128)(2,1)S(1)}, bf16[32,1024]{1,0:T(8,128)(2,1)S(1)}, u32[]{:S(2)}, u32[]{:S(2)}) collective-permute-start(bf16[32,1024]{1,0:T(8,128)(2,1)S(1)} %reduce_sum.12), channel_id=1, source_target_pairs={{0,128},{64,192},{128,0},{192,64},{1,129},{65,193},{129,1},{193,65... | collective-permute-start | bytes 196616 | tf_op jit(solution)/shard_map/ppermute | solution.py:230
